TPU v7x, 768 devices: a whole 4x8x12 slice. The times are simulated.
768 devices in a mesh: grid: 12 (over x, z_hi), state: 64 (over z_lo, y, core).
Axes of the slice: x: 4, y: 8, z: 12 (z_hi: 3, z_lo: 4; z = z_hi * 4 + z_lo), core: 2. Of those that a mesh axis runs over, the one named last changes fastest.
Arguments:
- orbitals: bfloat16 [512, 72, 16, 32], P('state', 'grid'), may hold values from -6 to 6
- potential: float32 [72, 16, 32], P('grid'), may hold values from -1.5 to 0.5
- occupation: float32 [512], P('state'), may hold values from 0.1 to 2
Outputs:
- subspace_energy: float32 [512, 512], P('state')
- subspace_gram: float32 [512, 512], P('state')
- density: float32 [72, 16, 32], P('grid')
All inputs are finite; a program needn't handle non-finite values.
Results may differ from a plain program's by a relative error of at most 0.0021.
Values may be sent and summed in bfloat16 or wider, within the bound.
No kernel may reach another device: no remote copies, remote signals or barrier semaphores. Data moves between devices by JAX's collectives and lax.ppermute only.
A program may use at most 32 MiB of HBM per device.

v0:
```python
import jax
import jax.numpy as jnp
from jax import lax
from jax.sharding import PartitionSpec as P

NS = 512
RADIUS = 6
DEGREE = 4


stencil_weights = (
    -5369.0 / 1800.0,
    12.0 / 7.0,
    -15.0 / 56.0,
    10.0 / 189.0,
    -1.0 / 112.0,
    2.0 / 1925.0,
    -1.0 / 16632.0,
)
cut_low = 1.0
cut_high = 12.0
contract_cells = (((1,), (1,)), ((), ()))
highest = lax.Precision.HIGHEST


def extended(cells, sides, width):
    for axis, dim in sides:
        count = lax.axis_size(axis)
        head = lax.slice_in_dim(cells, 0, width, axis=dim)
        tail = lax.slice_in_dim(cells, cells.shape[dim] - width, cells.shape[dim], axis=dim)
        cells = jnp.concatenate(
            [
                lax.ppermute(tail, axis, [(i, (i + 1) % count) for i in range(count)]),
                cells,
                lax.ppermute(head, axis, [((i + 1) % count, i) for i in range(count)]),
            ],
            axis=dim,
        )
    return cells


def circulant(count):
    rows_index = lax.broadcasted_iota(jnp.int32, (count, count), 0)
    cols_index = lax.broadcasted_iota(jnp.int32, (count, count), 1)
    offset = (cols_index - rows_index) % count
    matrix = jnp.where(offset == 0, stencil_weights[0], 0.0).astype(jnp.float32)
    for reach in range(1, RADIUS + 1):
        hit = (offset == reach) | (offset == count - reach)
        matrix = matrix + jnp.where(hit, stencil_weights[reach], 0.0).astype(jnp.float32)
    return matrix


def plane_band(planes):
    rows_index = lax.broadcasted_iota(jnp.int32, (planes, planes + 2 * RADIUS), 0)
    cols_index = lax.broadcasted_iota(jnp.int32, (planes, planes + 2 * RADIUS), 1)
    offset = jnp.abs(cols_index - rows_index - RADIUS)
    matrix = jnp.zeros((planes, planes + 2 * RADIUS), jnp.float32)
    for reach in range(0, RADIUS + 1):
        matrix = matrix + jnp.where(offset == reach, stencil_weights[reach], 0.0).astype(
            jnp.float32
        )
    return matrix


def hamiltonian(slab_block, potential):
    widened = extended(slab_block, (("grid", 1),), RADIUS).astype(jnp.float32)
    planes = slab_block.shape[1]
    middle = widened[:, RADIUS : RADIUS + planes]
    along_z = jnp.einsum("zp,spxy->szxy", plane_band(planes), widened, precision=highest)
    along_x = jnp.einsum("szxy,xw->szwy", middle, circulant(slab_block.shape[2]), precision=highest)
    along_y = jnp.einsum("szxy,yw->szxw", middle, circulant(slab_block.shape[3]), precision=highest)
    laplace = along_z + along_x + along_y
    return -0.5 * laplace + potential[None] * middle


def body(orbitals, potential, occupation):
    states = orbitals.shape[0]
    points = orbitals.shape[1] * orbitals.shape[2] * orbitals.shape[3]
    total_points = points * lax.axis_size("grid")
    centre = 0.5 * (cut_high + cut_low)
    spread = 0.5 * (cut_high - cut_low)

    def scaled(slab_block):
        return (
            hamiltonian(slab_block, potential) - centre * slab_block.astype(jnp.float32)
        ) / spread

    previous = orbitals
    current = scaled(orbitals).astype(jnp.bfloat16)
    for degree_index in range(1, DEGREE):
        following = (2.0 * scaled(current) - previous.astype(jnp.float32)).astype(jnp.bfloat16)
        previous = current
        current = following
    applied = hamiltonian(current, potential).astype(jnp.bfloat16)
    flat_orbit = current.reshape(states, points)
    flat_applied = applied.reshape(states, points)
    panel_in = lax.all_gather(flat_orbit, "state", axis=0, tiled=True)
    block_energy = lax.dot_general(
        flat_applied, panel_in, contract_cells, preferred_element_type=jnp.float32
    )
    block_gram = lax.dot_general(
        flat_orbit, panel_in, contract_cells, preferred_element_type=jnp.float32
    )
    stacked = jnp.stack((block_energy, block_gram), axis=1)
    summed = lax.psum(stacked, "grid")
    inverse_cells = 1.0 / total_points
    energy = summed[:, 0] * inverse_cells
    gram = summed[:, 1] * inverse_cells
    squares = jnp.square(current.astype(jnp.float32))
    partial_density = jnp.sum(occupation[:, None, None, None] * squares, axis=0)
    density = lax.psum(partial_density, "state") / NS
    return (energy, gram, density)


def solution(mesh):
    placed = (P("state", "grid", None, None), P("grid", None, None), P("state"))
    return jax.shard_map(
        body,
        mesh=mesh,
        in_specs=placed,
        out_specs=(P("state", None), P("state", None), P("grid", None, None)),
        check_vma=False,
    )
```

profile of v0, /device:TPU:2, one launch (start us, length us, event | category | flops | bytes accessed | tf_op | source)
XLA Modules:
  0.0 525.0 jit_solution(10904957461110701121)
XLA Ops:
  7.2 1.0 copy.54
  8.2 10.9 %collective-permute-start = (bf16[8,6,16,32]{3,1,2,0:T(8,128)(2,1)S(1)}, bf16[8,6,16,32]{3,1,2,0:T(8,128)(2,1)S(1)}, u32[]{:S(2)}, u32[]{:S(2)}) collective-permute-start(bf16[8,6,16,32]{3,1,2,0:T(8,128)(2,1)S(1)} %copy.54), channel_id=1, source_target_pairs={{0,64},{64,128},{128,192},{192,256},{256,320},{320,384},{384,448},... | collective-permute-start | bytes 147464 | tf_op jit(solution)/shard_map/ppermute | solution.py:33
  19.1 5.5 %collective-permute-start.1 = (bf16[8,6,16,32]{3,1,2,0:T(8,128)(2,1)S(1)}, bf16[8,6,16,32]{3,1,2,0:T(8,128)(2,1)S(1)}, u32[]{:S(2)}, u32[]{:S(2)}) collective-permute-start(bf16[8,6,16,32]{3,1,2,0:T(8,128)(2,1)S(1)} %copy.54), channel_id=1, source_target_pairs={{64,0},{128,64},{192,128},{256,192},{320,256},{384,320},{448,384},... | collective-permute-start | bytes 147464 | tf_op jit(solution)/shard_map/ppermute | solution.py:35
  24.7 1.3 fusion.83
  26.0 1.2 fusion.94
  27.3 2.2 collective-permute-done
  29.4 16.6 %collective-permute-done.1 = bf16[8,6,16,32]{3,1,2,0:T(8,128)(2,1)S(1)} collective-permute-done((bf16[8,6,16,32]{3,1,2,0:T(8,128)(2,1)S(1)}, bf16[8,6,16,32]{3,1,2,0:T(8,128)(2,1)S(1)}, u32[]{:S(2)}, u32[]{:S(2)}) %collective-permute-start.1) | collective-permute-done | bytes 49184 | tf_op jit(solution)/shard_map/ppermute | solution.py:35
  46.0 0.9 fusion.31
  47.3 12.3 %collective-permute-start.2 = (bf16[8,6,16,32]{3,1,2,0:T(8,128)(2,1)S(1)}, bf16[8,6,16,32]{3,1,2,0:T(8,128)(2,1)S(1)}, u32[]{:S(2)}, u32[]{:S(2)}) collective-permute-start(bf16[8,6,16,32]{3,1,2,0:T(8,128)(2,1)S(1)} %fusion.31), channel_id=1, source_target_pairs={{0,64},{64,128},{128,192},{192,256},{256,320},{320,384},{384,448},... | collective-permute-start | bytes 147464 | tf_op jit(solution)/shard_map/ppermute | solution.py:33
  59.6 1.9 collective-permute-start.3
  61.8 5.0 collective-permute-done.2
  66.8 20.8 %collective-permute-done.3 = bf16[8,6,16,32]{3,1,2,0:T(8,128)(2,1)S(1)} collective-permute-done((bf16[8,6,16,32]{3,1,2,0:T(8,128)(2,1)S(1)}, bf16[8,6,16,32]{3,1,2,0:T(8,128)(2,1)S(1)}, u32[]{:S(2)}, u32[]{:S(2)}) %collective-permute-start.3) | collective-permute-done | bytes 49184 | tf_op jit(solution)/shard_map/ppermute | solution.py:35
  87.6 1.0 fusion.34
  88.9 1.9 collective-permute-start.4
  90.9 8.7 %collective-permute-start.5 = (bf16[8,6,16,32]{3,1,2,0:T(8,128)(2,1)S(1)}, bf16[8,6,16,32]{3,1,2,0:T(8,128)(2,1)S(1)}, u32[]{:S(2)}, u32[]{:S(2)}) collective-permute-start(bf16[8,6,16,32]{3,1,2,0:T(8,128)(2,1)S(1)} %fusion.34), channel_id=1, source_target_pairs={{64,0},{128,64},{192,128},{256,192},{320,256},{384,320},{448,384},... | collective-permute-start | bytes 147464 | tf_op jit(solution)/shard_map/ppermute | solution.py:35
  99.9 20.1 %collective-permute-done.4 = bf16[8,6,16,32]{3,1,2,0:T(8,128)(2,1)S(1)} collective-permute-done((bf16[8,6,16,32]{3,1,2,0:T(8,128)(2,1)S(1)}, bf16[8,6,16,32]{3,1,2,0:T(8,128)(2,1)S(1)}, u32[]{:S(2)}, u32[]{:S(2)}) %collective-permute-start.4) | collective-permute-done | bytes 49184 | tf_op jit(solution)/shard_map/ppermute | solution.py:33
  120.0 0.9 fusion.33
  121.3 1.9 collective-permute-start.6
  123.3 8.7 %collective-permute-start.7 = (bf16[8,6,16,32]{3,1,2,0:T(8,128)(2,1)S(1)}, bf16[8,6,16,32]{3,1,2,0:T(8,128)(2,1)S(1)}, u32[]{:S(2)}, u32[]{:S(2)}) collective-permute-start(bf16[8,6,16,32]{3,1,2,0:T(8,128)(2,1)S(1)} %fusion.33), channel_id=1, source_target_pairs={{64,0},{128,64},{192,128},{256,192},{320,256},{384,320},{448,384},... | collective-permute-start | bytes 147464 | tf_op jit(solution)/shard_map/ppermute | solution.py:35
  132.3 11.8 %collective-permute-done.6 = bf16[8,6,16,32]{3,1,2,0:T(8,128)(2,1)S(1)} collective-permute-done((bf16[8,6,16,32]{3,1,2,0:T(8,128)(2,1)S(1)}, bf16[8,6,16,32]{3,1,2,0:T(8,128)(2,1)S(1)}, u32[]{:S(2)}, u32[]{:S(2)}) %collective-permute-start.6) | collective-permute-done | bytes 49184 | tf_op jit(solution)/shard_map/ppermute | solution.py:33
  144.2 2.8 collective-permute-done.7
  147.0 1.0 fusion.62
  148.0 0.8 reshape.19
  148.9 1.9 collective-permute-start.8
  150.8 9.3 %collective-permute-start.9 = (bf16[8,6,16,32]{3,1,2,0:T(8,128)(2,1)S(1)}, bf16[8,6,16,32]{3,1,2,0:T(8,128)(2,1)S(1)}, u32[]{:S(2)}, u32[]{:S(2)}) collective-permute-start(bf16[8,6,16,32]{3,1,2,0:T(8,128)(2,1)S(1)} %get-tuple-element.9), channel_id=1, source_target_pairs={{64,0},{128,64},{192,128},{256,192},{320,256},{384,320},{448,384},... | collective-permute-start | bytes 147464 | tf_op jit(solution)/shard_map/ppermute | solution.py:35
  160.1 265.5 %psum.15 = f32[6,16,32]{2,0,1:T(8,128)S(1)} all-reduce(f32[6,16,32]{2,0,1:T(8,128)S(1)} %get-tuple-element.8), channel_id=1, replica_groups=mesh['grid'=12,'state'=64] {'state'}, use_global_device_ids=true, to_apply=%region_2.3 | all-reduce | flops 3072 | bytes 24576 | tf_op jit(solution)/shard_map/psum | solution.py:111
  426.3 0.6 copy.79
  427.0 0.9 fusion.35
  428.1 2.9 convolution_bitcast_fusion.5
  431.1 0.9 convolution_bitcast_fusion.6
  432.0 85.5 %psum.14 = f32[8,2,512]{2,0,1:T(8,128)S(1)} all-reduce(f32[8,2,512]{2,0,1:T(8,128)S(1)} %pad_maximum_fusion), channel_id=1, replica_groups=mesh['grid'=12,'state'=64] {'grid'}, use_global_device_ids=true, to_apply=%region_0.1 | all-reduce | flops 8192 | bytes 65536 | tf_op jit(solution)/shard_map/psum | solution.py:105
  517.5 0.6 fusion.76
  (30 shorter events, 3.0 us)
Async XLA Ops:
  7.2 20.0 %copy-start.3 = (f32[6,16,32]{2,1,0:T(8,128)S(1)}, f32[6,16,32]{2,1,0:T(8,128)}, u32[]{:S(2)}) copy-start(f32[6,16,32]{2,1,0:T(8,128)} %param.4) | copy-start | bytes 36868
  7.2 420.9 %all-gather.2.cloned.1.call-start = ((), (), s32[]{:S(2)}) async-start(), calls=%async_computation | async-start | bytes 3194880 | tf_op jit(solution)/shard_map/all_gather | solution.py:97
  8.2 21.2 %collective-permute-start = (bf16[8,6,16,32]{3,1,2,0:T(8,128)(2,1)S(1)}, bf16[8,6,16,32]{3,1,2,0:T(8,128)(2,1)S(1)}, u32[]{:S(2)}, u32[]{:S(2)}) collective-permute-start(bf16[8,6,16,32]{3,1,2,0:T(8,128)(2,1)S(1)} %copy.54), channel_id=1, source_target_pairs={{0,64},{64,128},{128,192},{192,256},{256,320},{320,384},{384,448},... | collective-permute-start | bytes 147464 | tf_op jit(solution)/shard_map/ppermute | solution.py:33
  19.1 26.9 %collective-permute-start.1 = (bf16[8,6,16,32]{3,1,2,0:T(8,128)(2,1)S(1)}, bf16[8,6,16,32]{3,1,2,0:T(8,128)(2,1)S(1)}, u32[]{:S(2)}, u32[]{:S(2)}) collective-permute-start(bf16[8,6,16,32]{3,1,2,0:T(8,128)(2,1)S(1)} %copy.54), channel_id=1, source_target_pairs={{64,0},{128,64},{192,128},{256,192},{320,256},{384,320},{448,384},... | collective-permute-start | bytes 147464 | tf_op jit(solution)/shard_map/ppermute | solution.py:35
  27.2 60.4 %copy-start.1 = (bf16[8,6,16,32]{3,2,1,0:T(8,128)(2,1)S(1)}, bf16[8,6,16,32]{3,2,1,0:T(8,128)(2,1)}, u32[]{:S(2)}) copy-start(bf16[8,6,16,32]{3,2,1,0:T(8,128)(2,1)} %param.3) | copy-start | bytes 147460
  47.3 19.5 %collective-permute-start.2 = (bf16[8,6,16,32]{3,1,2,0:T(8,128)(2,1)S(1)}, bf16[8,6,16,32]{3,1,2,0:T(8,128)(2,1)S(1)}, u32[]{:S(2)}, u32[]{:S(2)}) collective-permute-start(bf16[8,6,16,32]{3,1,2,0:T(8,128)(2,1)S(1)} %fusion.31), channel_id=1, source_target_pairs={{0,64},{64,128},{128,192},{192,256},{256,320},{320,384},{384,448},... | collective-permute-start | bytes 147464 | tf_op jit(solution)/shard_map/ppermute | solution.py:33
  59.6 28.0 %collective-permute-start.3 = (bf16[8,6,16,32]{3,1,2,0:T(8,128)(2,1)S(1)}, bf16[8,6,16,32]{3,1,2,0:T(8,128)(2,1)S(1)}, u32[]{:S(2)}, u32[]{:S(2)}) collective-permute-start(bf16[8,6,16,32]{3,1,2,0:T(8,128)(2,1)S(1)} %fusion.31), channel_id=1, source_target_pairs={{64,0},{128,64},{192,128},{256,192},{320,256},{384,320},{448,384},... | collective-permute-start | bytes 147464 | tf_op jit(solution)/shard_map/ppermute | solution.py:35
  88.9 31.1 %collective-permute-start.4 = (bf16[8,6,16,32]{3,1,2,0:T(8,128)(2,1)S(1)}, bf16[8,6,16,32]{3,1,2,0:T(8,128)(2,1)S(1)}, u32[]{:S(2)}, u32[]{:S(2)}) collective-permute-start(bf16[8,6,16,32]{3,1,2,0:T(8,128)(2,1)S(1)} %fusion.34), channel_id=1, source_target_pairs={{0,64},{64,128},{128,192},{192,256},{256,320},{320,384},{384,448},... | collective-permute-start | bytes 147464 | tf_op jit(solution)/shard_map/ppermute | solution.py:33
  90.9 29.2 %collective-permute-start.5 = (bf16[8,6,16,32]{3,1,2,0:T(8,128)(2,1)S(1)}, bf16[8,6,16,32]{3,1,2,0:T(8,128)(2,1)S(1)}, u32[]{:S(2)}, u32[]{:S(2)}) collective-permute-start(bf16[8,6,16,32]{3,1,2,0:T(8,128)(2,1)S(1)} %fusion.34), channel_id=1, source_target_pairs={{64,0},{128,64},{192,128},{256,192},{320,256},{384,320},{448,384},... | collective-permute-start | bytes 147464 | tf_op jit(solution)/shard_map/ppermute | solution.py:35
  99.9 47.0 %copy-start.4 = (f32[8]{0:T(128)S(1)}, f32[8]{0:T(128)}, u32[]{:S(2)}) copy-start(f32[8]{0:T(128)} %param.5) | copy-start | bytes 100
  121.3 22.8 %collective-permute-start.6 = (bf16[8,6,16,32]{3,1,2,0:T(8,128)(2,1)S(1)}, bf16[8,6,16,32]{3,1,2,0:T(8,128)(2,1)S(1)}, u32[]{:S(2)}, u32[]{:S(2)}) collective-permute-start(bf16[8,6,16,32]{3,1,2,0:T(8,128)(2,1)S(1)} %fusion.33), channel_id=1, source_target_pairs={{0,64},{64,128},{128,192},{192,256},{256,320},{320,384},{384,448},... | collective-permute-start | bytes 147464 | tf_op jit(solution)/shard_map/ppermute | solution.py:33
  123.3 23.7 %collective-permute-start.7 = (bf16[8,6,16,32]{3,1,2,0:T(8,128)(2,1)S(1)}, bf16[8,6,16,32]{3,1,2,0:T(8,128)(2,1)S(1)}, u32[]{:S(2)}, u32[]{:S(2)}) collective-permute-start(bf16[8,6,16,32]{3,1,2,0:T(8,128)(2,1)S(1)} %fusion.33), channel_id=1, source_target_pairs={{64,0},{128,64},{192,128},{256,192},{320,256},{384,320},{448,384},... | collective-permute-start | bytes 147464 | tf_op jit(solution)/shard_map/ppermute | solution.py:35
  148.9 278.1 %collective-permute-start.8 = (bf16[8,6,16,32]{3,1,2,0:T(8,128)(2,1)S(1)}, bf16[8,6,16,32]{3,1,2,0:T(8,128)(2,1)S(1)}, u32[]{:S(2)}, u32[]{:S(2)}) collective-permute-start(bf16[8,6,16,32]{3,1,2,0:T(8,128)(2,1)S(1)} %get-tuple-element.9), channel_id=1, source_target_pairs={{0,64},{64,128},{128,192},{192,256},{256,320},{320,384},{384,448},... | collective-permute-start | bytes 147464 | tf_op jit(solution)/shard_map/ppermute | solution.py:33
  150.8 276.1 %collective-permute-start.9 = (bf16[8,6,16,32]{3,1,2,0:T(8,128)(2,1)S(1)}, bf16[8,6,16,32]{3,1,2,0:T(8,128)(2,1)S(1)}, u32[]{:S(2)}, u32[]{:S(2)}) collective-permute-start(bf16[8,6,16,32]{3,1,2,0:T(8,128)(2,1)S(1)} %get-tuple-element.9), channel_id=1, source_target_pairs={{64,0},{128,64},{192,128},{256,192},{320,256},{384,320},{448,384},... | collective-permute-start | bytes 147464 | tf_op jit(solution)/shard_map/ppermute | solution.py:35
  427.0 1.2 copy-start.2
  428.1 3.0 copy-start
Sparse Core Ops, SparseCore 0:
  149.0 129.5 all-gather.1
where the time goes:
time: 525 us
  blocking collectives  351 us (67%)
  waiting for transfers between devices  79.3 us (15%)
  starting transfers between devices  63.2 us (12%)
  between operations  14.3 us (3%)
  matrix products  13.7 us (3%)
    psum x1, blocking collectives, body(): density = lax.psum(partial_density, 'state') / NS  266 us
    psum x1, blocking collectives, body(): summed = lax.psum(stacked, 'grid')  85.5 us
    ppermute x5, waiting for transfers between devices, extended(): lax.ppermute(head, axis, [((i + 1) % count, i) for i in range(count)])  40.2 us
    ppermute x5, waiting for transfers between devices, extended(): lax.ppermute(tail, axis, [(i, (i + 1) % count) for i in range(count)])  39.1 us
    ppermute x5, starting transfers between devices, extended(): lax.ppermute(head, axis, [((i + 1) % count, i) for i in range(count)])  34.2 us
    ppermute x5, starting transfers between devices, extended(): lax.ppermute(tail, axis, [(i, (i + 1) % count) for i in range(count)])  28.9 us
  transfers between devices with their start and end apart: 11, of which 7 were waited for; matrix products, arithmetic and copies ran while one was open for 1% of the time, Pallas kernels for 0%

commit v1 on v0

v1 whole, which is shorter than its diff:
```python
import jax
import jax.numpy as jnp
import numpy as np
from jax import lax
from jax.experimental import pallas as pl
from jax.experimental.pallas import tpu as pltpu
from jax.sharding import Mesh
from jax.sharding import PartitionSpec as P

NS = 512
RADIUS = 6
DEGREE = 4
NX = 16
NY = 32
NZ = 72
PLANE = NX * NY
SLABS = 12
THICK = NZ // SLABS

stencil_weights = (
    -5369.0 / 1800.0,
    12.0 / 7.0,
    -15.0 / 56.0,
    10.0 / 189.0,
    -1.0 / 112.0,
    2.0 / 1925.0,
    -1.0 / 16632.0,
)
cut_low = 1.0
cut_high = 12.0
centre = 0.5 * (cut_high + cut_low)
spread = 0.5 * (cut_high - cut_low)
bf16 = jnp.bfloat16
f32 = jnp.float32


def ring(count):
    line = np.zeros((count, count))
    rows = np.arange(count)
    for reach in range(1, RADIUS + 1):
        line[rows, (rows + reach) % count] += -0.5 * stencil_weights[reach]
        line[rows, (rows - reach) % count] += -0.5 * stencil_weights[reach]
    return line


def halves(matrix):
    high = matrix.astype(np.float32).astype(bf16)
    low = (matrix - high.astype(np.float64)).astype(np.float32).astype(bf16)
    return high, low


plane_high, plane_low = halves(
    np.kron(ring(NX), np.eye(NY)) + np.kron(np.eye(NX), ring(NY))
)
depth_high, depth_low = halves(np.kron(np.eye(2), ring(NZ)))


def unpacking():
    matrix = np.zeros((4 * NZ, 4 * NZ), np.float32)
    for slab in range(SLABS):
        for plane in range(THICK):
            for state in range(2):
                z = slab * THICK + plane
                base = slab * 4 * THICK + plane
                matrix[state * NZ + z, base + state * THICK] = 1.0
                matrix[(2 + state) * NZ + z, base + 2 * THICK] = 1.0
                matrix[(2 + state) * NZ + z, base + 3 * THICK] = 1.0
    return matrix.astype(bf16)


unpack = unpacking()


def product(a, b):
    return lax.dot_general(a, b, (((1,), (0,)), ((), ())), preferred_element_type=f32)


def filter_kernel(place, occupied, slabs, unpack_rows, high_xy, low_xy, high_z, low_z, out):
    count = 2 * NZ
    everything = product(unpack_rows[...], slabs[...])
    first = everything[:count]
    diagonal = everything[count:] - 1.5 * stencil_weights[0]
    shifted = diagonal - centre

    def hop(v):
        return (
            product(v, high_xy[...])
            + product(v, low_xy[...])
            + product(high_z[...], v)
            + product(low_z[...], v)
        )

    previous = first
    current = ((hop(first.astype(bf16)) + shifted * first) * (1.0 / spread)).astype(bf16)
    for _ in range(1, DEGREE):
        wide = current.astype(f32)
        following = (hop(current) + shifted * wide) * (2.0 / spread) - previous
        previous = wide
        current = following.astype(bf16)
    applied = (hop(current) + diagonal * current.astype(f32)).astype(bf16)

    row = lax.broadcasted_iota(jnp.int32, (48, count), 0)
    col = lax.broadcasted_iota(jnp.int32, (48, count), 1)
    group = (row >> 1) & 7
    z = THICK * (3 * (group >> 1) + place[1]) + 3 * (group & 1) + (row >> 4)
    pick = jnp.where(col == (row & 1) * NZ + z, 1.0, 0.0).astype(bf16)
    filtered_rows = product(pick, current).astype(bf16)
    applied_rows = product(pick, applied).astype(bf16)
    for lane_block in range(4):
        lanes = slice(lane_block * 128, lane_block * 128 + 128)
        for p in range(3):
            rows = slice(p * 16, p * 16 + 16)
            target = slice(lane_block * 16, lane_block * 16 + 16)
            out[target, p * 128 : p * 128 + 128] = filtered_rows[rows, lanes]
            out[target, 512 + p * 128 : 640 + p * 128] = applied_rows[rows, lanes]
    state = lax.broadcasted_iota(jnp.int32, (64, 128), 0) & 1
    lane = lax.broadcasted_iota(jnp.int32, (64, 128), 1)
    block = jnp.zeros((64, 128), f32)
    for piece in range(3):
        for k in range(2):
            value = occupied[piece * 8 + 2 * place[0] + k]
            block = jnp.where((lane == piece) & (state == k), value, block)
    out[:, 384:512] = block.astype(bf16)


def tile_kernel(own, gathered, out):
    row = lax.broadcasted_iota(jnp.int32, (NS, NS), 0)
    col = lax.broadcasted_iota(jnp.int32, (NS, NS), 1)
    source = ((((row >> 3) & 1) * 4 + ((row >> 1) & 3)) * 32 + (row >> 4)) * 2 + (row & 1)
    order = jnp.where(col == source, 1.0, 0.0).astype(bf16)
    ordered = product(order, gathered[...])
    states = ordered[:, :384]
    occupied = ordered[:, 384:385] + ordered[:, 385:386] + ordered[:, 386:387]
    density = jnp.sum(occupied * (states * states), axis=0, keepdims=True) * (1.0 / NS)

    row = lax.broadcasted_iota(jnp.int32, (128, 128), 0)
    col = lax.broadcasted_iota(jnp.int32, (128, 128), 1)
    source = ((row >> 1) & 1) * 64 + (row >> 2) * 2 + (row & 1)
    interleave = jnp.where(col == source, 1.0, 0.0).astype(bf16)
    stacked = jnp.concatenate([own[:, 512:896], own[:, 0:384]], axis=0)
    left = product(interleave, stacked).astype(bf16)
    out[:, 0:512] = lax.dot_general(
        left, states.astype(bf16), (((1,), (1,)), ((), ())), preferred_element_type=f32
    )
    kind = row & 3
    block = jnp.zeros((128, 128), f32)
    for p in range(3):
        block = jnp.where(kind == p, density[:, p * 128 : p * 128 + 128], block)
    out[:, 512:640] = block


def exchange(array, axes):
    return lax.all_to_all(array, axes, 0, 0, tiled=True)


def body(orbitals, potential, occupation):
    x = lax.axis_index("x")
    place = jnp.stack([x, lax.axis_index("zh")]).astype(jnp.int32)

    high = lax.reduce_precision(potential, 8, 7)
    low = potential - high
    wells = jnp.stack([high.astype(bf16), low.astype(bf16)]).reshape(1, 2 * THICK, PLANE)
    slabs = jnp.concatenate(
        [orbitals.reshape(4, 2 * THICK, PLANE), jnp.broadcast_to(wells, (4, 2 * THICK, PLANE))],
        axis=1,
    )
    slabs = jnp.broadcast_to(slabs[:, None], (4, 3, 4 * THICK, PLANE)).reshape(SLABS, 4 * THICK, PLANE)
    slabs = exchange(slabs, ("x", "zh")).reshape(4 * NZ, PLANE)

    occ_high = lax.reduce_precision(occupation, 8, 7)
    occ_rest = occupation - occ_high
    occ_mid = lax.reduce_precision(occ_rest, 8, 7)
    occupied = jnp.concatenate([occ_high, occ_mid, occ_rest - occ_mid])

    smem = pl.BlockSpec(memory_space=pltpu.SMEM)
    vmem = pl.BlockSpec(memory_space=pltpu.VMEM)
    params = pltpu.CompilerParams(vmem_limit_bytes=24 * 1024 * 1024)
    send = pl.pallas_call(
        filter_kernel,
        out_shape=jax.ShapeDtypeStruct((64, 896), bf16),
        in_specs=[smem, smem] + [vmem] * 6,
        out_specs=vmem,
        compiler_params=params,
        name="chebyshev",
    )(place, occupied, slabs, unpack, plane_high, plane_low, depth_high, depth_low)

    own = exchange(send.reshape(32, 2, 896), ("zl", "y")).reshape(64, 896)
    shared = jnp.broadcast_to(own[None, :, :512], (4, 64, 512))
    gathered = exchange(shared, "x").reshape(256, 512)
    gathered = lax.all_gather(gathered, "c", axis=0, tiled=True)

    partial = pl.pallas_call(
        tile_kernel,
        out_shape=jax.ShapeDtypeStruct((128, 640), f32),
        in_specs=[vmem] * 2,
        out_specs=vmem,
        compiler_params=params,
        name="tiles",
    )(own, gathered)

    parts = exchange(partial.reshape(32, 4, 640), ("zl", "y"))
    rows = jnp.sum(parts[:, :, :512], axis=0)
    cells = parts.reshape(4, 4, 2, 4, 640)[:, :, :, :3, 512:]
    cells = lax.dynamic_index_in_dim(cells, x, axis=1, keepdims=False)
    density = jnp.transpose(cells, (1, 2, 0, 3)).reshape(THICK, NX, NY)

    rows = exchange(jnp.broadcast_to(rows[None], (SLABS, 4, 512)), ("x", "zh"))
    rows = jnp.sum(rows.reshape(4, 3, 4, 512), axis=1) * (1.0 / (NZ * PLANE))
    return rows[:, :2].reshape(8, NS), rows[:, 2:].reshape(8, NS), density


def solution(mesh):
    fine = Mesh(mesh.devices.reshape(4, 3, 4, 8, 2), ("x", "zh", "zl", "y", "c"))
    grid, state = ("x", "zh"), ("zl", "y", "c")
    return jax.shard_map(
        body,
        mesh=fine,
        in_specs=(P(state, grid, None, None), P(grid, None, None), P(state)),
        out_specs=(P(state, None), P(state, None), P(grid, None, None)),
        check_vma=False,
    )
```

time: 525 us -> 107 us (0.20)
  the two profiles are of different devices: /device:TPU:2 before, /device:TPU:8 now
where the time goes in v1:
time: 107 us
  blocking collectives  49.6 us (46%)
  waiting for transfers between devices  26.3 us (25%)
  starting transfers between devices  20.8 us (19%)
  local copies, waits for them, and re-layouts  4.5 us (4%)
  Pallas kernels  3.38 us (3%)
  other arithmetic  1.14 us (1%)
    all_to_all x3, blocking collectives, exchange(): return lax.all_to_all(array, axes, 0, 0, tiled=True)  47.4 us
    all_to_all x2, waiting for transfers between devices, exchange(): return lax.all_to_all(array, axes, 0, 0, tiled=True)  26.3 us
    all_to_all x2, starting transfers between devices, exchange(): return lax.all_to_all(array, axes, 0, 0, tiled=True)  20.8 us
    pallas_call x1, Pallas kernels, body(): pl.pallas_call(filter_kernel, out_shape=jax.ShapeDtypeStruct((64, 896), b...  2.69 us
    all_gather x1, blocking collectives, body(): gathered = lax.all_gather(gathered, 'c', axis=0, tiled=True)  2.17 us
  transfers between devices with their start and end apart: 2, of which 2 were waited for; matrix products, arithmetic and copies ran while one was open for 1% of the time, Pallas kernels for 0%

profile of v1, /device:TPU:8, one launch (start us, length us, event | category | flops | bytes accessed | tf_op | source)
XLA Modules:
  0.0 106.6 jit_solution(14745131262454122295)
XLA Ops:
  0.6 0.0 copy-start.5
  0.6 0.8 fusion.2
  1.5 0.1 broadcast_in_dim.10
  1.6 0.0 copy-done.5
  1.6 0.0 copy-start.3
  1.6 0.0 copy-start.4
  1.7 0.2 reshape.47
  1.8 0.0 copy-start.2
  1.9 0.0 copy-start.1
  1.9 0.0 copy-start
  1.9 0.7 broadcast_in_dim.12
  2.7 16.4 %all-to-all-start = ((bf16[12,24,512]{2,1,0:T(8,128)(2,1)}), bf16[12,24,512]{2,1,0:T(8,128)(2,1)S(1)}, u32[]{:S(2)}, u32[]{:S(2)}) async-start(bf16[12,24,512]{2,1,0:T(8,128)(2,1)} %bitcast.4), calls=%async_computation | async-start | bytes 589824 | tf_op jit(solution)/shard_map/all_to_all | solution.py:153
  19.1 0.0 copy-start.6
  19.1 0.1 pad_add_fusion.place
  19.2 0.6 copy-done.6
  19.8 0.1 pad_maximum_fusion.2.occupied
  19.9 15.6 %all-to-all-done = bf16[12,24,512]{2,1,0:T(8,128)(2,1)S(1)} async-done(((bf16[12,24,512]{2,1,0:T(8,128)(2,1)}), bf16[12,24,512]{2,1,0:T(8,128)(2,1)S(1)}, u32[]{:S(2)}, u32[]{:S(2)}) %all-to-all-start) | async-done | bytes 294944 | tf_op jit(solution)/shard_map/all_to_all | solution.py:153
  35.5 0.0 copy-done.4
  35.5 2.7 %chebyshev.1 = bf16[64,896]{1,0:T(8,128)(2,1)S(1)} custom-call(s32[2]{0:T(128)S(1)} %pad_add_fusion.place, f32[24]{0:T(128)S(1)} %pad_maximum_fusion.2.occupied, bf16[288,512]{1,0:T(8,128)(2,1)S(1)} %bitcast.20, bf16[288,288]{1,0:T(8,128)(2,1)S(1)} %copy-done.2, bf16[512,512]{1,0:T(8,128)(2,1)S(1)} %copy-done.1, bf16[512,512]{1,0:T(8,128)(2,1)S(1)} %copy-done, ...), custom_call_target="tpu_custom_call" | custom-call | tf_op jit(solution)/shard_map/chebyshev/pallas_call | solution.py:178
  38.3 20.6 %all_to_all.25 = bf16[32,2,896]{2,1,0:T(2,128)(2,1)S(1)} all-to-all(bf16[32,2,896]{2,1,0:T(2,128)(2,1)S(1)} %reshape.50), channel_id=1, replica_groups=mesh['x'=4,'zh'=3,'zl'=4,'y'=8,'c'=2] {'zl','y'}, dimensions={0} | all-to-all | bytes 229376 | tf_op jit(solution)/shard_map/all_to_all | solution.py:153
  59.0 9.1 %all_to_all.26 = bf16[4,64,512]{2,1,0:T(8,128)(2,1)S(1)} all-to-all(bf16[4,64,512]{2,1,0:T(8,128)(2,1)S(1)} %broadcast_in_dim.13), channel_id=1, replica_groups=mesh['x'=4,'zh'=3,'zl'=4,'y'=8,'c'=2] {'x'}, dimensions={0} | all-to-all | bytes 524288 | tf_op jit(solution)/shard_map/all_to_all | solution.py:153
  68.1 2.2 %all_gather.3.gathered = bf16[512,512]{1,0:T(8,128)(2,1)S(1)} all-gather(bf16[256,512]{1,0:T(8,128)(2,1)S(1)} %bitcast.22), channel_id=1, replica_groups=mesh['x'=4,'zh'=3,'zl'=4,'y'=8,'c'=2] {'c'}, dimensions={0}, use_global_device_ids=true | all-gather | bytes 786432 | tf_op jit(solution)/shard_map/all_gather | solution.py:190
  70.2 0.7 tiles.1
  71.0 0.1 reshape.53
  71.1 17.7 %all_to_all.27 = f32[32,4,640]{2,1,0:T(4,128)S(1)} all-to-all(f32[32,4,640]{2,1,0:T(4,128)S(1)} %reshape.53), channel_id=1, replica_groups=mesh['x'=4,'zh'=3,'zl'=4,'y'=8,'c'=2] {'zl','y'}, dimensions={0} | all-to-all | bytes 655360 | tf_op jit(solution)/shard_map/all_to_all | solution.py:153
  88.8 0.1 slice_reduce_fusion
  88.8 0.6 broadcast_in_dim.14
  89.5 4.4 %all-to-all-start.4 = ((f32[12,4,512]{2,1,0:T(4,128)}), f32[12,4,512]{2,1,0:T(4,128)S(1)}, u32[]{:S(2)}, u32[]{:S(2)}) async-start(f32[12,4,512]{2,1,0:T(4,128)} %broadcast_in_dim.14), calls=%async_computation.4 | async-start | bytes 196608 | tf_op jit(solution)/shard_map/all_to_all | solution.py:153
  93.9 0.7 reshape.58
  94.6 10.7 %all-to-all-done.4 = f32[12,4,512]{2,1,0:T(4,128)S(1)} async-done(((f32[12,4,512]{2,1,0:T(4,128)}), f32[12,4,512]{2,1,0:T(4,128)S(1)}, u32[]{:S(2)}, u32[]{:S(2)}) %all-to-all-start.4) | async-done | bytes 98336 | tf_op jit(solution)/shard_map/all_to_all | solution.py:153
  105.4 0.6 reshape.56
  106.0 0.6 reshape.55
  (18 shorter events, 0.3 us)
Async XLA Ops:
  0.6 1.0 copy-start.5
  1.6 33.9 %copy-start.3 = (bf16[144,144]{1,0:T(8,128)(2,1)S(1)}, bf16[144,144]{1,0:T(8,128)(2,1)}, u32[]{:S(2)}) copy-start(bf16[144,144]{1,0:T(8,128)(2,1)} %constant.33.clone.low_z) | copy-start | bytes 124420
  1.6 33.9 %copy-start.4 = (bf16[144,144]{1,0:T(8,128)(2,1)S(1)}, bf16[144,144]{1,0:T(8,128)(2,1)}, u32[]{:S(2)}) copy-start(bf16[144,144]{1,0:T(8,128)(2,1)} %constant.32.clone.high_z) | copy-start | bytes 124420
  1.8 33.7 %copy-start.2 = (bf16[288,288]{1,0:T(8,128)(2,1)S(1)}, bf16[288,288]{1,0:T(8,128)(2,1)}, u32[]{:S(2)}) copy-start(bf16[288,288]{1,0:T(8,128)(2,1)} %constant.29.clone.unpack_rows) | copy-start | bytes 497668
  1.9 33.6 %copy-start.1 = (bf16[512,512]{1,0:T(8,128)(2,1)S(1)}, bf16[512,512]{1,0:T(8,128)(2,1)}, u32[]{:S(2)}) copy-start(bf16[512,512]{1,0:T(8,128)(2,1)} %constant.30.clone.high_xy) | copy-start | bytes 1572868
  1.9 33.6 %copy-start = (bf16[512,512]{1,0:T(8,128)(2,1)S(1)}, bf16[512,512]{1,0:T(8,128)(2,1)}, u32[]{:S(2)}) copy-start(bf16[512,512]{1,0:T(8,128)(2,1)} %constant.31.clone.low_xy) | copy-start | bytes 1572868
  2.7 32.8 %all-to-all-start = ((bf16[12,24,512]{2,1,0:T(8,128)(2,1)}), bf16[12,24,512]{2,1,0:T(8,128)(2,1)S(1)}, u32[]{:S(2)}, u32[]{:S(2)}) async-start(bf16[12,24,512]{2,1,0:T(8,128)(2,1)} %bitcast.4), calls=%async_computation | async-start | bytes 589824 | tf_op jit(solution)/shard_map/all_to_all | solution.py:153
  19.1 0.7 copy-start.6
  89.5 15.9 %all-to-all-start.4 = ((f32[12,4,512]{2,1,0:T(4,128)}), f32[12,4,512]{2,1,0:T(4,128)S(1)}, u32[]{:S(2)}, u32[]{:S(2)}) async-start(f32[12,4,512]{2,1,0:T(4,128)} %broadcast_in_dim.14), calls=%async_computation.4 | async-start | bytes 196608 | tf_op jit(solution)/shard_map/all_to_all | solution.py:153

commit v2 on v1

--- a/solution.py
+++ b/solution.py
@@ -16,6 +16,9 @@
 PLANE = NX * NY
 SLABS = 12
 THICK = NZ // SLABS
+CELLS = NZ * PLANE // 32
+SHARED = CELLS + 128
+PACKED = SHARED + CELLS
 
 stencil_weights = (
     -5369.0 / 1800.0,
@@ -52,19 +55,29 @@
 plane_high, plane_low = halves(
     np.kron(ring(NX), np.eye(NY)) + np.kron(np.eye(NX), ring(NY))
 )
-depth_high, depth_low = halves(np.kron(np.eye(2), ring(NZ)))
+
+row_z = np.array(
+    [
+        THICK * (3 * (group >> 1) + hi) + 3 * (group & 1) + p
+        for hi in range(3)
+        for p in range(3)
+        for group in range(8)
+        for _ in range(2)
+    ]
+)
+row_state = np.arange(2 * NZ) % 2
+depth_high, depth_low = halves(
+    ring(NZ)[row_z][:, row_z] * (row_state[:, None] == row_state[None, :])
+)
 
 
 def unpacking():
     matrix = np.zeros((4 * NZ, 4 * NZ), np.float32)
-    for slab in range(SLABS):
-        for plane in range(THICK):
-            for state in range(2):
-                z = slab * THICK + plane
-                base = slab * 4 * THICK + plane
-                matrix[state * NZ + z, base + state * THICK] = 1.0
-                matrix[(2 + state) * NZ + z, base + 2 * THICK] = 1.0
-                matrix[(2 + state) * NZ + z, base + 3 * THICK] = 1.0
+    rows = np.arange(2 * NZ)
+    base = (row_z // THICK) * 4 * THICK + row_z % THICK
+    matrix[rows, base + row_state * THICK] = 1.0
+    matrix[2 * NZ + rows, base + 2 * THICK] = 1.0
+    matrix[2 * NZ + rows, base + 3 * THICK] = 1.0
     return matrix.astype(bf16)
 
 
@@ -99,20 +112,13 @@
         current = following.astype(bf16)
     applied = (hop(current) + diagonal * current.astype(f32)).astype(bf16)
 
-    row = lax.broadcasted_iota(jnp.int32, (48, count), 0)
-    col = lax.broadcasted_iota(jnp.int32, (48, count), 1)
-    group = (row >> 1) & 7
-    z = THICK * (3 * (group >> 1) + place[1]) + 3 * (group & 1) + (row >> 4)
-    pick = jnp.where(col == (row & 1) * NZ + z, 1.0, 0.0).astype(bf16)
-    filtered_rows = product(pick, current).astype(bf16)
-    applied_rows = product(pick, applied).astype(bf16)
     for lane_block in range(4):
         lanes = slice(lane_block * 128, lane_block * 128 + 128)
-        for p in range(3):
-            rows = slice(p * 16, p * 16 + 16)
-            target = slice(lane_block * 16, lane_block * 16 + 16)
-            out[target, p * 128 : p * 128 + 128] = filtered_rows[rows, lanes]
-            out[target, 512 + p * 128 : 640 + p * 128] = applied_rows[rows, lanes]
+        target = slice(lane_block * 16, lane_block * 16 + 16)
+        for q in range(9):
+            rows = slice(q * 16, q * 16 + 16)
+            out[target, q * 128 : q * 128 + 128] = current[rows, lanes]
+            out[target, SHARED + q * 128 : SHARED + q * 128 + 128] = applied[rows, lanes]
     state = lax.broadcasted_iota(jnp.int32, (64, 128), 0) & 1
     lane = lax.broadcasted_iota(jnp.int32, (64, 128), 1)
     block = jnp.zeros((64, 128), f32)
@@ -120,27 +126,33 @@
         for k in range(2):
             value = occupied[piece * 8 + 2 * place[0] + k]
             block = jnp.where((lane == piece) & (state == k), value, block)
-    out[:, 384:512] = block.astype(bf16)
-
-
-def tile_kernel(own, gathered, out):
+    out[:, CELLS:SHARED] = block.astype(bf16)
+
+
+def tile_kernel(place, own, mine, other, out):
     row = lax.broadcasted_iota(jnp.int32, (NS, NS), 0)
     col = lax.broadcasted_iota(jnp.int32, (NS, NS), 1)
-    source = ((((row >> 3) & 1) * 4 + ((row >> 1) & 3)) * 32 + (row >> 4)) * 2 + (row & 1)
+    core = ((row >> 3) & 1) ^ place[2]
+    source = ((core * 4 + ((row >> 1) & 3)) * 32 + (row >> 4)) * 2 + (row & 1)
     order = jnp.where(col == source, 1.0, 0.0).astype(bf16)
-    ordered = product(order, gathered[...])
-    states = ordered[:, :384]
-    occupied = ordered[:, 384:385] + ordered[:, 385:386] + ordered[:, 386:387]
-    density = jnp.sum(occupied * (states * states), axis=0, keepdims=True) * (1.0 / NS)
+    gathered = jnp.concatenate([mine[...], other[...]], axis=0)
+    ordered = product(order, gathered)
+    states = ordered[:, :CELLS].astype(bf16)
+    occupied = ordered[:, CELLS:SHARED]
+    occupied = occupied[:, 0:1] + occupied[:, 1:2] + occupied[:, 2:3]
+    third = CELLS // 3
+    slab = jnp.where(place[1] == 0, ordered[:, :third], ordered[:, third : 2 * third])
+    slab = jnp.where(place[1] == 2, ordered[:, 2 * third : CELLS], slab)
+    density = jnp.sum(occupied * (slab * slab), axis=0, keepdims=True) * (1.0 / NS)
 
     row = lax.broadcasted_iota(jnp.int32, (128, 128), 0)
     col = lax.broadcasted_iota(jnp.int32, (128, 128), 1)
     source = ((row >> 1) & 1) * 64 + (row >> 2) * 2 + (row & 1)
     interleave = jnp.where(col == source, 1.0, 0.0).astype(bf16)
-    stacked = jnp.concatenate([own[:, 512:896], own[:, 0:384]], axis=0)
+    stacked = jnp.concatenate([own[:, SHARED:PACKED], own[:, 0:CELLS]], axis=0)
     left = product(interleave, stacked).astype(bf16)
     out[:, 0:512] = lax.dot_general(
-        left, states.astype(bf16), (((1,), (1,)), ((), ())), preferred_element_type=f32
+        left, states, (((1,), (1,)), ((), ())), preferred_element_type=f32
     )
     kind = row & 3
     block = jnp.zeros((128, 128), f32)
@@ -155,7 +167,7 @@
 
 def body(orbitals, potential, occupation):
     x = lax.axis_index("x")
-    place = jnp.stack([x, lax.axis_index("zh")]).astype(jnp.int32)
+    place = jnp.stack([x, lax.axis_index("zh"), lax.axis_index("c")]).astype(jnp.int32)
 
     high = lax.reduce_precision(potential, 8, 7)
     low = potential - high
@@ -177,26 +189,26 @@
     params = pltpu.CompilerParams(vmem_limit_bytes=24 * 1024 * 1024)
     send = pl.pallas_call(
         filter_kernel,
-        out_shape=jax.ShapeDtypeStruct((64, 896), bf16),
+        out_shape=jax.ShapeDtypeStruct((64, PACKED), bf16),
         in_specs=[smem, smem] + [vmem] * 6,
         out_specs=vmem,
         compiler_params=params,
         name="chebyshev",
     )(place, occupied, slabs, unpack, plane_high, plane_low, depth_high, depth_low)
 
-    own = exchange(send.reshape(32, 2, 896), ("zl", "y")).reshape(64, 896)
-    shared = jnp.broadcast_to(own[None, :, :512], (4, 64, 512))
-    gathered = exchange(shared, "x").reshape(256, 512)
-    gathered = lax.all_gather(gathered, "c", axis=0, tiled=True)
+    own = exchange(send.reshape(32, 2, PACKED), ("zl", "y")).reshape(64, PACKED)
+    shared = jnp.broadcast_to(own[None, :, :SHARED], (4, 64, SHARED))
+    mine = exchange(shared, "x").reshape(256, SHARED)
+    other = lax.ppermute(mine, "c", [(0, 1), (1, 0)])
 
     partial = pl.pallas_call(
         tile_kernel,
         out_shape=jax.ShapeDtypeStruct((128, 640), f32),
-        in_specs=[vmem] * 2,
+        in_specs=[smem] + [vmem] * 3,
         out_specs=vmem,
         compiler_params=params,
         name="tiles",
-    )(own, gathered)
+    )(place, own, mine, other)
 
     parts = exchange(partial.reshape(32, 4, 640), ("zl", "y"))
     rows = jnp.sum(parts[:, :, :512], axis=0)
@@ -204,8 +216,7 @@
     cells = lax.dynamic_index_in_dim(cells, x, axis=1, keepdims=False)
     density = jnp.transpose(cells, (1, 2, 0, 3)).reshape(THICK, NX, NY)
 
-    rows = exchange(jnp.broadcast_to(rows[None], (SLABS, 4, 512)), ("x", "zh"))
-    rows = jnp.sum(rows.reshape(4, 3, 4, 512), axis=1) * (1.0 / (NZ * PLANE))
+    rows = exchange(jnp.broadcast_to(rows[None], (4, 4, 512)), "x") * (1.0 / (NZ * PLANE))
     return rows[:, :2].reshape(8, NS), rows[:, 2:].reshape(8, NS), density
 
 

time: 107 us -> 112 us (1.047)
  blocking collectives: 49.6 us -> 35.2 us
  waiting for transfers between devices: 26.3 us -> 36 us
  starting transfers between devices: 20.8 us -> 28.7 us
    all_to_all x3 -> x2, blocking collectives: 47.4 us -> 35.2 us  [exchange(): return lax.all_to_all(array, axes, 0, 0, tiled=True)]
    all_to_all x2 -> x3, waiting for transfers between devices: 26.3 us -> 33.9 us  [exchange(): return lax.all_to_all(array, axes, 0, 0, tiled=True)]
    all_to_all x2 -> x3, starting transfers between devices: 20.8 us -> 26.8 us  [exchange(): return lax.all_to_all(array, axes, 0, 0, tiled=True)]
    all_gather x1 -> x0, blocking collectives: 2.17 us -> none  [body(): gathered = lax.all_gather(gathered, 'c', axis=0, tiled=True)]
    ppermute x0 -> x1, waiting for transfers between devices: none -> 2.06 us  [body(): other = lax.ppermute(mine, 'c', [(0, 1), (1, 0)])]
    ppermute x0 -> x1, starting transfers between devices: none -> 1.91 us  [body(): other = lax.ppermute(mine, 'c', [(0, 1), (1, 0)])]
    pallas_call x1, Pallas kernels: 0.69 us -> 1.89 us  [body(): pl.pallas_call(tile_kernel, out_shape=jax.ShapeDtypeStruct((128, 640), f3...]
  transfers between devices with their start and end apart: 2 -> 4, of which waited for: 2 -> 4; matrix products, arithmetic and copies ran while one was open for 1% -> 1% of each run, Pallas kernels for 0% -> 0%
where the time goes in v2:
time: 112 us
  waiting for transfers between devices  36 us (32%)
  blocking collectives  35.2 us (31%)
  starting transfers between devices  28.7 us (26%)
  local copies, waits for them, and re-layouts  5.35 us (5%)
  Pallas kernels  4.46 us (4%)
    all_to_all x2, blocking collectives, exchange(): return lax.all_to_all(array, axes, 0, 0, tiled=True)  35.2 us
    all_to_all x3, waiting for transfers between devices, exchange(): return lax.all_to_all(array, axes, 0, 0, tiled=True)  33.9 us
    all_to_all x3, starting transfers between devices, exchange(): return lax.all_to_all(array, axes, 0, 0, tiled=True)  26.8 us
    pallas_call x1, Pallas kernels, body(): pl.pallas_call(filter_kernel, out_shape=jax.ShapeDtypeStruct((64, PACKED)...  2.57 us
  transfers between devices with their start and end apart: 4, of which 4 were waited for; matrix products, arithmetic and copies ran while one was open for 1% of the time, Pallas kernels for 0%

profile of v2, /device:TPU:8, one launch (start us, length us, event | category | flops | bytes accessed | tf_op | source)
XLA Modules:
  0.0 111.7 jit_solution(18436649798589747212)
XLA Ops:
  0.6 0.8 fusion.2
  1.5 0.1 broadcast_in_dim.10
  1.6 0.0 copy-start.3
  1.6 0.0 copy-start.4
  1.7 0.2 reshape.44
  1.8 0.0 copy-start.2
  1.9 0.0 copy-start.1
  1.9 0.0 copy-start
  1.9 0.7 broadcast_in_dim.12
  2.7 16.4 %all-to-all-start = ((bf16[12,24,512]{2,1,0:T(8,128)(2,1)}), bf16[12,24,512]{2,1,0:T(8,128)(2,1)S(1)}, u32[]{:S(2)}, u32[]{:S(2)}) async-start(bf16[12,24,512]{2,1,0:T(8,128)(2,1)} %bitcast.5), calls=%async_computation | async-start | bytes 589824 | tf_op jit(solution)/shard_map/all_to_all | solution.py:165
  19.1 0.1 pad_add_fusion.place
  19.2 0.6 copy-done.6
  19.8 0.1 pad_maximum_fusion.2.occupied
  19.8 15.6 %all-to-all-done = bf16[12,24,512]{2,1,0:T(8,128)(2,1)S(1)} async-done(((bf16[12,24,512]{2,1,0:T(8,128)(2,1)}), bf16[12,24,512]{2,1,0:T(8,128)(2,1)S(1)}, u32[]{:S(2)}, u32[]{:S(2)}) %all-to-all-start) | async-done | bytes 294944 | tf_op jit(solution)/shard_map/all_to_all | solution.py:165
  35.5 2.6 %chebyshev.1 = bf16[64,2432]{1,0:T(8,128)(2,1)S(1)} custom-call(s32[3]{0:T(128)S(1)} %pad_add_fusion.place, f32[24]{0:T(128)S(1)} %pad_maximum_fusion.2.occupied, bf16[288,512]{1,0:T(8,128)(2,1)S(1)} %bitcast.22, bf16[288,288]{1,0:T(8,128)(2,1)S(1)} %copy-done.2, bf16[512,512]{1,0:T(8,128)(2,1)S(1)} %copy-done.1, bf16[512,512]{1,0:T(8,128)(2,1)S(1)} %copy-done, ...), custom_call_target="tpu_custom_call" | custom-call | tf_op jit(solution)/shard_map/chebyshev/pallas_call | solution.py:190
  38.1 0.1 reshape.47
  38.2 24.0 %all_to_all.25 = bf16[32,2,2432]{2,1,0:T(2,128)(2,1)S(1)} all-to-all(bf16[32,2,2432]{2,1,0:T(2,128)(2,1)S(1)} %reshape.47), channel_id=1, replica_groups=mesh['x'=4,'zh'=3,'zl'=4,'y'=8,'c'=2] {'zl','y'}, dimensions={0} | all-to-all | bytes 622592 | tf_op jit(solution)/shard_map/all_to_all | solution.py:165
  62.2 0.1 reshape.48.own
  62.4 11.2 %all_to_all.26 = bf16[4,64,1280]{2,1,0:T(8,128)(2,1)S(1)} all-to-all(bf16[4,64,1280]{2,1,0:T(8,128)(2,1)S(1)} %broadcast_in_dim.13), channel_id=1, replica_groups=mesh['x'=4,'zh'=3,'zl'=4,'y'=8,'c'=2] {'x'}, dimensions={0} | all-to-all | bytes 1310720 | tf_op jit(solution)/shard_map/all_to_all | solution.py:165
  73.6 1.9 %collective-permute-start = (bf16[256,1280]{1,0:T(8,128)(2,1)S(1)}, bf16[256,1280]{1,0:T(8,128)(2,1)S(1)}, u32[]{:S(2)}, u32[]{:S(2)}) collective-permute-start(bf16[256,1280]{1,0:T(8,128)(2,1)S(1)} %bitcast.20), channel_id=1, source_target_pairs={{0,1},{1,0},{2,3},{3,2},{4,5},{5,4},{6,7},{7,6},{8,9},{9,8},{10,11... | collective-permute-start | bytes 1966088 | tf_op jit(solution)/shard_map/ppermute | solution.py:202
  75.5 2.1 %collective-permute-done.other = bf16[256,1280]{1,0:T(8,128)(2,1)S(1)} collective-permute-done((bf16[256,1280]{1,0:T(8,128)(2,1)S(1)}, bf16[256,1280]{1,0:T(8,128)(2,1)S(1)}, u32[]{:S(2)}, u32[]{:S(2)}) %collective-permute-start) | collective-permute-done | bytes 655392 | tf_op jit(solution)/shard_map/ppermute | solution.py:202
  77.6 1.9 %tiles.1 = f32[128,640]{1,0:T(8,128)S(1)} custom-call(s32[3]{0:T(128)S(1)} %pad_add_fusion.place, bf16[64,2432]{1,0:T(8,128)(2,1)S(1)} %reshape.48.own, bf16[256,1280]{1,0:T(8,128)(2,1)S(1)} %bitcast.21, bf16[256,1280]{1,0:T(8,128)(2,1)S(1)} %collective-permute-done.other), custom_call_target="tpu_custom_call" | custom-call | tf_op jit(solution)/shard_map/tiles/pallas_call | solution.py:204
  79.5 0.8 reshape.50
  80.3 7.1 %all-to-all-start.3 = ((f32[32,4,640]{2,1,0:T(4,128)}), f32[32,4,640]{2,1,0:T(4,128)S(1)}, u32[]{:S(2)}, u32[]{:S(2)}) async-start(f32[32,4,640]{2,1,0:T(4,128)} %reshape.50), calls=%async_computation.3 | async-start | bytes 655360 | tf_op jit(solution)/shard_map/all_to_all | solution.py:165
  87.4 13.6 %all-to-all-done.3 = f32[32,4,640]{2,1,0:T(4,128)S(1)} async-done(((f32[32,4,640]{2,1,0:T(4,128)}), f32[32,4,640]{2,1,0:T(4,128)S(1)}, u32[]{:S(2)}, u32[]{:S(2)}) %all-to-all-start.3) | async-done | bytes 327712 | tf_op jit(solution)/shard_map/all_to_all | solution.py:165
  101.0 0.1 slice_reduce_fusion
  101.1 0.6 broadcast_in_dim.14
  101.7 3.3 %all-to-all-start.4 = ((f32[4,4,512]{2,1,0:T(4,128)}), f32[4,4,512]{2,1,0:T(4,128)S(1)}, u32[]{:S(2)}, u32[]{:S(2)}) async-start(f32[4,4,512]{2,1,0:T(4,128)} %broadcast_in_dim.14), calls=%async_computation.4 | async-start | bytes 65536 | tf_op jit(solution)/shard_map/all_to_all | solution.py:165
  105.0 0.7 reshape.54
  105.7 4.7 %all-to-all-done.4 = f32[4,4,512]{2,1,0:T(4,128)S(1)} async-done(((f32[4,4,512]{2,1,0:T(4,128)}), f32[4,4,512]{2,1,0:T(4,128)S(1)}, u32[]{:S(2)}, u32[]{:S(2)}) %all-to-all-start.4) | async-done | bytes 32800 | tf_op jit(solution)/shard_map/all_to_all | solution.py:165
  110.4 0.6 reshape.52
  111.0 0.6 reshape.51
  (19 shorter events, 0.2 us)
Async XLA Ops:
  0.6 1.0 copy-start.5
  1.6 33.9 %copy-start.3 = (bf16[144,144]{1,0:T(8,128)(2,1)S(1)}, bf16[144,144]{1,0:T(8,128)(2,1)}, u32[]{:S(2)}) copy-start(bf16[144,144]{1,0:T(8,128)(2,1)} %constant.37.clone.low_z) | copy-start | bytes 124420
  1.6 33.8 %copy-start.4 = (bf16[144,144]{1,0:T(8,128)(2,1)S(1)}, bf16[144,144]{1,0:T(8,128)(2,1)}, u32[]{:S(2)}) copy-start(bf16[144,144]{1,0:T(8,128)(2,1)} %constant.36.clone.high_z) | copy-start | bytes 124420
  1.8 33.6 %copy-start.2 = (bf16[288,288]{1,0:T(8,128)(2,1)S(1)}, bf16[288,288]{1,0:T(8,128)(2,1)}, u32[]{:S(2)}) copy-start(bf16[288,288]{1,0:T(8,128)(2,1)} %constant.33.clone.unpack_rows) | copy-start | bytes 497668
  1.9 33.6 %copy-start.1 = (bf16[512,512]{1,0:T(8,128)(2,1)S(1)}, bf16[512,512]{1,0:T(8,128)(2,1)}, u32[]{:S(2)}) copy-start(bf16[512,512]{1,0:T(8,128)(2,1)} %constant.34.clone.high_xy) | copy-start | bytes 1572868
  1.9 33.6 %copy-start = (bf16[512,512]{1,0:T(8,128)(2,1)S(1)}, bf16[512,512]{1,0:T(8,128)(2,1)}, u32[]{:S(2)}) copy-start(bf16[512,512]{1,0:T(8,128)(2,1)} %constant.35.clone.low_xy) | copy-start | bytes 1572868
  2.7 32.8 %all-to-all-start = ((bf16[12,24,512]{2,1,0:T(8,128)(2,1)}), bf16[12,24,512]{2,1,0:T(8,128)(2,1)S(1)}, u32[]{:S(2)}, u32[]{:S(2)}) async-start(bf16[12,24,512]{2,1,0:T(8,128)(2,1)} %bitcast.5), calls=%async_computation | async-start | bytes 589824 | tf_op jit(solution)/shard_map/all_to_all | solution.py:165
  19.1 0.7 copy-start.6
  73.6 4.0 %collective-permute-start = (bf16[256,1280]{1,0:T(8,128)(2,1)S(1)}, bf16[256,1280]{1,0:T(8,128)(2,1)S(1)}, u32[]{:S(2)}, u32[]{:S(2)}) collective-permute-start(bf16[256,1280]{1,0:T(8,128)(2,1)S(1)} %bitcast.20), channel_id=1, source_target_pairs={{0,1},{1,0},{2,3},{3,2},{4,5},{5,4},{6,7},{7,6},{8,9},{9,8},{10,11... | collective-permute-start | bytes 1966088 | tf_op jit(solution)/shard_map/ppermute | solution.py:202
  80.3 20.7 %all-to-all-start.3 = ((f32[32,4,640]{2,1,0:T(4,128)}), f32[32,4,640]{2,1,0:T(4,128)S(1)}, u32[]{:S(2)}, u32[]{:S(2)}) async-start(f32[32,4,640]{2,1,0:T(4,128)} %reshape.50), calls=%async_computation.3 | async-start | bytes 655360 | tf_op jit(solution)/shard_map/all_to_all | solution.py:165
  101.7 8.7 %all-to-all-start.4 = ((f32[4,4,512]{2,1,0:T(4,128)}), f32[4,4,512]{2,1,0:T(4,128)S(1)}, u32[]{:S(2)}, u32[]{:S(2)}) async-start(f32[4,4,512]{2,1,0:T(4,128)} %broadcast_in_dim.14), calls=%async_computation.4 | async-start | bytes 65536 | tf_op jit(solution)/shard_map/all_to_all | solution.py:165

commit v3 on v1

--- a/solution.py
+++ b/solution.py
@@ -75,7 +75,7 @@
     return lax.dot_general(a, b, (((1,), (0,)), ((), ())), preferred_element_type=f32)
 
 
-def filter_kernel(place, occupied, slabs, unpack_rows, high_xy, low_xy, high_z, low_z, out):
+def filter_kernel(occupation, slabs, unpack_rows, high_xy, low_xy, high_z, low_z, out):
     count = 2 * NZ
     everything = product(unpack_rows[...], slabs[...])
     first = everything[:count]
@@ -102,7 +102,7 @@
     row = lax.broadcasted_iota(jnp.int32, (48, count), 0)
     col = lax.broadcasted_iota(jnp.int32, (48, count), 1)
     group = (row >> 1) & 7
-    z = THICK * (3 * (group >> 1) + place[1]) + 3 * (group & 1) + (row >> 4)
+    z = THICK * (3 * (group >> 1) + lax.axis_index("zh")) + 3 * (group & 1) + (row >> 4)
     pick = jnp.where(col == (row & 1) * NZ + z, 1.0, 0.0).astype(bf16)
     filtered_rows = product(pick, current).astype(bf16)
     applied_rows = product(pick, applied).astype(bf16)
@@ -115,11 +115,15 @@
             out[target, 512 + p * 128 : 640 + p * 128] = applied_rows[rows, lanes]
     state = lax.broadcasted_iota(jnp.int32, (64, 128), 0) & 1
     lane = lax.broadcasted_iota(jnp.int32, (64, 128), 1)
+    held = lax.broadcasted_iota(jnp.int32, (1, 8), 1)
+    mine = 2 * lax.axis_index("x")
     block = jnp.zeros((64, 128), f32)
-    for piece in range(3):
-        for k in range(2):
-            value = occupied[piece * 8 + 2 * place[0] + k]
-            block = jnp.where((lane == piece) & (state == k), value, block)
+    for k in range(2):
+        value = jnp.sum(jnp.where(held == mine + k, occupation[...], 0.0), axis=1, keepdims=True)
+        for piece in range(3):
+            part = value.astype(bf16).astype(f32)
+            value = value - part
+            block = jnp.where((lane == piece) & (state == k), part, block)
     out[:, 384:512] = block.astype(bf16)
 
 
@@ -139,14 +143,43 @@
     interleave = jnp.where(col == source, 1.0, 0.0).astype(bf16)
     stacked = jnp.concatenate([own[:, 512:896], own[:, 0:384]], axis=0)
     left = product(interleave, stacked).astype(bf16)
-    out[:, 0:512] = lax.dot_general(
+    tiles = lax.dot_general(
         left, states.astype(bf16), (((1,), (1,)), ((), ())), preferred_element_type=f32
     )
+    out[:, 0:512] = tiles.astype(bf16)
     kind = row & 3
     block = jnp.zeros((128, 128), f32)
     for p in range(3):
         block = jnp.where(kind == p, density[:, p * 128 : p * 128 + 128], block)
-    out[:, 512:640] = block
+    high = block.astype(bf16)
+    out[:, 512:640] = high
+    out[:, 640:768] = (block - high.astype(f32)).astype(bf16)
+
+
+def sum_kernel(parts, rows, density):
+    row = lax.broadcasted_iota(jnp.int32, (4 * SLABS, 128), 0)
+    col = lax.broadcasted_iota(jnp.int32, (4 * SLABS, 128), 1)
+    adder = jnp.where((row & 3) == (col & 3), 1.0, 0.0).astype(bf16)
+    rows[...] = product(adder, parts[:, 0:512])
+    row = lax.broadcasted_iota(jnp.int32, (8, 128), 0)
+    col = lax.broadcasted_iota(jnp.int32, (8, 128), 1)
+    half = jnp.where(row >= 3, 1, 0)
+    for lane_block in range(4):
+        sender = lane_block * 8 + 2 * lax.axis_index("x") + half
+        pick = jnp.where((col == sender * 4 + row - 3 * half) & (row < THICK), 1.0, 0.0).astype(bf16)
+        lanes = slice(lane_block * 128, lane_block * 128 + 128)
+        density[:, lanes] = product(pick, parts[:, 512:640]) + product(pick, parts[:, 640:768])
+
+
+def final_kernel(rows, cells, energy, gram, density):
+    scale = 1.0 / (NZ * PLANE)
+    for x in range(4):
+        total = rows[12 * x : 12 * x + 4] + rows[12 * x + 4 : 12 * x + 8] + rows[12 * x + 8 : 12 * x + 12]
+        total = total * scale
+        energy[2 * x : 2 * x + 2] = total[0:2]
+        gram[2 * x : 2 * x + 2] = total[2:4]
+    for line in range(NX):
+        density[:, line, :] = cells[0:THICK, line * NY : line * NY + NY]
 
 
 def exchange(array, axes):
@@ -154,9 +187,6 @@
 
 
 def body(orbitals, potential, occupation):
-    x = lax.axis_index("x")
-    place = jnp.stack([x, lax.axis_index("zh")]).astype(jnp.int32)
-
     high = lax.reduce_precision(potential, 8, 7)
     low = potential - high
     wells = jnp.stack([high.astype(bf16), low.astype(bf16)]).reshape(1, 2 * THICK, PLANE)
@@ -167,22 +197,16 @@
     slabs = jnp.broadcast_to(slabs[:, None], (4, 3, 4 * THICK, PLANE)).reshape(SLABS, 4 * THICK, PLANE)
     slabs = exchange(slabs, ("x", "zh")).reshape(4 * NZ, PLANE)
 
-    occ_high = lax.reduce_precision(occupation, 8, 7)
-    occ_rest = occupation - occ_high
-    occ_mid = lax.reduce_precision(occ_rest, 8, 7)
-    occupied = jnp.concatenate([occ_high, occ_mid, occ_rest - occ_mid])
-
-    smem = pl.BlockSpec(memory_space=pltpu.SMEM)
     vmem = pl.BlockSpec(memory_space=pltpu.VMEM)
     params = pltpu.CompilerParams(vmem_limit_bytes=24 * 1024 * 1024)
     send = pl.pallas_call(
         filter_kernel,
         out_shape=jax.ShapeDtypeStruct((64, 896), bf16),
-        in_specs=[smem, smem] + [vmem] * 6,
+        in_specs=[vmem] * 7,
         out_specs=vmem,
         compiler_params=params,
         name="chebyshev",
-    )(place, occupied, slabs, unpack, plane_high, plane_low, depth_high, depth_low)
+    )(occupation.reshape(1, 8), slabs, unpack, plane_high, plane_low, depth_high, depth_low)
 
     own = exchange(send.reshape(32, 2, 896), ("zl", "y")).reshape(64, 896)
     shared = jnp.broadcast_to(own[None, :, :512], (4, 64, 512))
@@ -191,22 +215,39 @@
 
     partial = pl.pallas_call(
         tile_kernel,
-        out_shape=jax.ShapeDtypeStruct((128, 640), f32),
+        out_shape=jax.ShapeDtypeStruct((128, 768), bf16),
         in_specs=[vmem] * 2,
         out_specs=vmem,
         compiler_params=params,
         name="tiles",
     )(own, gathered)
 
-    parts = exchange(partial.reshape(32, 4, 640), ("zl", "y"))
-    rows = jnp.sum(parts[:, :, :512], axis=0)
-    cells = parts.reshape(4, 4, 2, 4, 640)[:, :, :, :3, 512:]
-    cells = lax.dynamic_index_in_dim(cells, x, axis=1, keepdims=False)
-    density = jnp.transpose(cells, (1, 2, 0, 3)).reshape(THICK, NX, NY)
-
-    rows = exchange(jnp.broadcast_to(rows[None], (SLABS, 4, 512)), ("x", "zh"))
-    rows = jnp.sum(rows.reshape(4, 3, 4, 512), axis=1) * (1.0 / (NZ * PLANE))
-    return rows[:, :2].reshape(8, NS), rows[:, 2:].reshape(8, NS), density
+    parts = exchange(partial.reshape(32, 4, 768), ("zl", "y")).reshape(128, 768)
+    rows, cells = pl.pallas_call(
+        sum_kernel,
+        out_shape=[
+            jax.ShapeDtypeStruct((4 * SLABS, NS), f32),
+            jax.ShapeDtypeStruct((8, PLANE), f32),
+        ],
+        in_specs=[vmem],
+        out_specs=[vmem] * 2,
+        compiler_params=params,
+        name="sums",
+    )(parts)
+
+    rows = exchange(rows.reshape(SLABS, 4, NS), ("x", "zh")).reshape(4 * SLABS, NS)
+    return pl.pallas_call(
+        final_kernel,
+        out_shape=[
+            jax.ShapeDtypeStruct((8, NS), f32),
+            jax.ShapeDtypeStruct((8, NS), f32),
+            jax.ShapeDtypeStruct((THICK, NX, NY), f32),
+        ],
+        in_specs=[vmem] * 2,
+        out_specs=[vmem] * 3,
+        compiler_params=params,
+        name="results",
+    )(rows, cells)
 
 
 def solution(mesh):

time: 107 us -> 103 us (0.963)
  blocking collectives: 49.6 us -> 95.4 us
  waiting for transfers between devices: 26.3 us -> 0 us
  starting transfers between devices: 20.8 us -> 0 us
  local copies, waits for them, and re-layouts: 4.5 us -> 1.27 us
    all_to_all x3 -> x5, blocking collectives: 47.4 us -> 93.3 us  [exchange(): return lax.all_to_all(array, axes, 0, 0, tiled=True)]
    all_to_all x2 -> x0, waiting for transfers between devices: 26.3 us -> none  [exchange(): return lax.all_to_all(array, axes, 0, 0, tiled=True)]
    all_to_all x2 -> x0, starting transfers between devices: 20.8 us -> none  [exchange(): return lax.all_to_all(array, axes, 0, 0, tiled=True)]
    reshape x4, local copies, waits for them, and re-layouts: 2.04 us -> 0.17 us  [the longest x2 0.1 us: body(): parts = exchange(partial.reshape(32, 4, 768), ('zl', 'y')).reshape(128, 768)]
  transfers between devices with their start and end apart: 2 -> 0, of which waited for: 2 -> 0; matrix products, arithmetic and copies ran while one was open for 1% -> 0% of each run, Pallas kernels for 0% -> 0%
where the time goes in v3:
time: 103 us; the launch traced here: 102 us
  blocking collectives  95.4 us (93%)
  Pallas kernels  3.82 us (4%)
  local copies, waits for them, and re-layouts  1.27 us (1%)
    all_to_all x5, blocking collectives, exchange(): return lax.all_to_all(array, axes, 0, 0, tiled=True)  93.3 us
    all_gather x1, blocking collectives, body(): gathered = lax.all_gather(gathered, 'c', axis=0, tiled=True)  2.17 us
    pallas_call x1, Pallas kernels, body(): pl.pallas_call(filter_kernel, out_shape=jax.ShapeDtypeStruct((64, 896), b...  2.15 us

profile of v3, /device:TPU:8, one launch (start us, length us, event | category | flops | bytes accessed | tf_op | source)
XLA Modules:
  0.0 102.2 jit_solution(791529589722588438)
XLA Ops:
  0.6 0.0 copy-start.6
  0.6 0.8 fusion.2
  1.5 0.1 broadcast_in_dim.8
  1.6 0.0 copy-done.6
  1.6 0.0 copy-start.3
  1.6 0.0 copy-start.4
  1.7 0.2 reshape.44
  1.8 0.0 copy-start.2
  1.9 0.0 copy-start.1
  1.9 0.0 copy-start
  2.0 32.8 %all_to_all.25 = bf16[12,24,512]{2,1,0:T(8,128)(2,1)S(1)} all-to-all(bf16[12,24,512]{2,1,0:T(8,128)(2,1)S(1)} %bitcast.14), channel_id=1, replica_groups=mesh['x'=4,'zh'=3,'zl'=4,'y'=8,'c'=2] {'x','zh'}, dimensions={0} | all-to-all | bytes 589824 | tf_op jit(solution)/shard_map/all_to_all | solution.py:186
  34.7 0.0 copy-start.5
  34.7 0.0 copy-done.3
  34.7 0.0 copy-done.4
  34.7 0.0 copy-done.2
  34.7 0.0 copy-done.1
  34.7 0.0 copy-done
  34.7 0.6 copy-done.5
  35.4 2.1 %chebyshev.1 = bf16[64,896]{1,0:T(8,128)(2,1)S(1)} custom-call(f32[1,8]{1,0:T(1,128)S(1)} %bitcast.13, bf16[288,512]{1,0:T(8,128)(2,1)S(1)} %bitcast.12, bf16[288,288]{1,0:T(8,128)(2,1)S(1)} %copy-done.2, bf16[512,512]{1,0:T(8,128)(2,1)S(1)} %copy-done.1, bf16[512,512]{1,0:T(8,128)(2,1)S(1)} %copy-done, bf16[144,144]{1,0:T(8,128)(2,1)S(1)} %copy-done.4, ...), custom_call_target="tpu_custom_call" | custom-call | tf_op jit(solution)/shard_map/chebyshev/pallas_call | solution.py:202
  37.6 20.6 %all_to_all.26 = bf16[32,2,896]{2,1,0:T(2,128)(2,1)S(1)} all-to-all(bf16[32,2,896]{2,1,0:T(2,128)(2,1)S(1)} %reshape.47), channel_id=1, replica_groups=mesh['x'=4,'zh'=3,'zl'=4,'y'=8,'c'=2] {'zl','y'}, dimensions={0} | all-to-all | bytes 229376 | tf_op jit(solution)/shard_map/all_to_all | solution.py:186
  58.3 9.1 %all_to_all.27 = bf16[4,64,512]{2,1,0:T(8,128)(2,1)S(1)} all-to-all(bf16[4,64,512]{2,1,0:T(8,128)(2,1)S(1)} %broadcast_in_dim.22), channel_id=1, replica_groups=mesh['x'=4,'zh'=3,'zl'=4,'y'=8,'c'=2] {'x'}, dimensions={0} | all-to-all | bytes 524288 | tf_op jit(solution)/shard_map/all_to_all | solution.py:186
  67.4 2.2 %all_gather.3.gathered = bf16[512,512]{1,0:T(8,128)(2,1)S(1)} all-gather(bf16[256,512]{1,0:T(8,128)(2,1)S(1)} %bitcast.15), channel_id=1, replica_groups=mesh['x'=4,'zh'=3,'zl'=4,'y'=8,'c'=2] {'c'}, dimensions={0}, use_global_device_ids=true | all-gather | bytes 786432 | tf_op jit(solution)/shard_map/all_gather | solution.py:214
  69.6 0.7 tiles.1
  70.3 0.1 reshape.50
  70.3 14.9 %all_to_all.28 = bf16[32,4,768]{2,1,0:T(4,128)(2,1)S(1)} all-to-all(bf16[32,4,768]{2,1,0:T(4,128)(2,1)S(1)} %reshape.50), channel_id=1, replica_groups=mesh['x'=4,'zh'=3,'zl'=4,'y'=8,'c'=2] {'zl','y'}, dimensions={0} | all-to-all | bytes 393216 | tf_op jit(solution)/shard_map/all_to_all | solution.py:186
  85.2 0.1 reshape.51.parts
  85.2 0.2 sums.1
  85.5 16.0 %all_to_all.29 = f32[12,4,512]{2,1,0:T(4,128)S(1)} all-to-all(f32[12,4,512]{2,1,0:T(4,128)S(1)} %reshape.52), channel_id=1, replica_groups=mesh['x'=4,'zh'=3,'zl'=4,'y'=8,'c'=2] {'x','zh'}, dimensions={0} | all-to-all | bytes 196608 | tf_op jit(solution)/shard_map/all_to_all | solution.py:186
  101.5 0.8 results.1
  (10 shorter events, 0.3 us)
Async XLA Ops:
  0.6 1.0 copy-start.6
  1.6 33.1 %copy-start.3 = (bf16[144,144]{1,0:T(8,128)(2,1)S(1)}, bf16[144,144]{1,0:T(8,128)(2,1)}, u32[]{:S(2)}) copy-start(bf16[144,144]{1,0:T(8,128)(2,1)} %constant.14.clone.low_z) | copy-start | bytes 124420
  1.6 33.1 %copy-start.4 = (bf16[144,144]{1,0:T(8,128)(2,1)S(1)}, bf16[144,144]{1,0:T(8,128)(2,1)}, u32[]{:S(2)}) copy-start(bf16[144,144]{1,0:T(8,128)(2,1)} %constant.13.clone.high_z) | copy-start | bytes 124420
  1.8 32.9 %copy-start.2 = (bf16[288,288]{1,0:T(8,128)(2,1)S(1)}, bf16[288,288]{1,0:T(8,128)(2,1)}, u32[]{:S(2)}) copy-start(bf16[288,288]{1,0:T(8,128)(2,1)} %constant.10.clone.unpack_rows) | copy-start | bytes 497668
  1.9 32.9 %copy-start.1 = (bf16[512,512]{1,0:T(8,128)(2,1)S(1)}, bf16[512,512]{1,0:T(8,128)(2,1)}, u32[]{:S(2)}) copy-start(bf16[512,512]{1,0:T(8,128)(2,1)} %constant.11.clone.high_xy) | copy-start | bytes 1572868
  1.9 32.8 %copy-start = (bf16[512,512]{1,0:T(8,128)(2,1)S(1)}, bf16[512,512]{1,0:T(8,128)(2,1)}, u32[]{:S(2)}) copy-start(bf16[512,512]{1,0:T(8,128)(2,1)} %constant.12.clone.low_xy) | copy-start | bytes 1572868
  34.7 0.7 copy-start.5

commit v4 on v3

--- a/solution.py
+++ b/solution.py
@@ -75,7 +75,11 @@
     return lax.dot_general(a, b, (((1,), (0,)), ((), ())), preferred_element_type=f32)
 
 
-def filter_kernel(occupation, slabs, unpack_rows, high_xy, low_xy, high_z, low_z, out):
+def filter_kernel(
+    occupation, slabs, unpack_rows, high_xy, low_xy, high_z, low_z, out, occupied, arrived
+):
+    fetch = pltpu.make_async_copy(occupation, occupied, arrived)
+    fetch.start()
     count = 2 * NZ
     everything = product(unpack_rows[...], slabs[...])
     first = everything[:count]
@@ -101,8 +105,8 @@
 
     row = lax.broadcasted_iota(jnp.int32, (48, count), 0)
     col = lax.broadcasted_iota(jnp.int32, (48, count), 1)
-    group = (row >> 1) & 7
-    z = THICK * (3 * (group >> 1) + lax.axis_index("zh")) + 3 * (group & 1) + (row >> 4)
+    slab = 3 * ((row >> 1) & 3) + lax.axis_index("zh")
+    z = THICK * slab + 3 * ((row >> 3) & 1) + (row >> 4)
     pick = jnp.where(col == (row & 1) * NZ + z, 1.0, 0.0).astype(bf16)
     filtered_rows = product(pick, current).astype(bf16)
     applied_rows = product(pick, applied).astype(bf16)
@@ -118,8 +122,9 @@
     held = lax.broadcasted_iota(jnp.int32, (1, 8), 1)
     mine = 2 * lax.axis_index("x")
     block = jnp.zeros((64, 128), f32)
+    fetch.wait()
     for k in range(2):
-        value = jnp.sum(jnp.where(held == mine + k, occupation[...], 0.0), axis=1, keepdims=True)
+        value = jnp.sum(jnp.where(held == mine + k, occupied[...], 0.0), axis=1, keepdims=True)
         for piece in range(3):
             part = value.astype(bf16).astype(f32)
             value = value - part
@@ -130,7 +135,7 @@
 def tile_kernel(own, gathered, out):
     row = lax.broadcasted_iota(jnp.int32, (NS, NS), 0)
     col = lax.broadcasted_iota(jnp.int32, (NS, NS), 1)
-    source = ((((row >> 3) & 1) * 4 + ((row >> 1) & 3)) * 32 + (row >> 4)) * 2 + (row & 1)
+    source = (((row >> 3) & 1) * 4 + (row >> 7)) * 64 + ((row >> 4) & 7) * 8 + (row & 7)
     order = jnp.where(col == source, 1.0, 0.0).astype(bf16)
     ordered = product(order, gathered[...])
     states = ordered[:, :384]
@@ -139,7 +144,7 @@
 
     row = lax.broadcasted_iota(jnp.int32, (128, 128), 0)
     col = lax.broadcasted_iota(jnp.int32, (128, 128), 1)
-    source = ((row >> 1) & 1) * 64 + (row >> 2) * 2 + (row & 1)
+    source = ((row >> 3) & 1) * 64 + (row >> 4) * 8 + (row & 7)
     interleave = jnp.where(col == source, 1.0, 0.0).astype(bf16)
     stacked = jnp.concatenate([own[:, 512:896], own[:, 0:384]], axis=0)
     left = product(interleave, stacked).astype(bf16)
@@ -147,37 +152,41 @@
         left, states.astype(bf16), (((1,), (1,)), ((), ())), preferred_element_type=f32
     )
     out[:, 0:512] = tiles.astype(bf16)
-    kind = row & 3
+    high = density.astype(bf16).astype(f32)
+    kind = row & 15
     block = jnp.zeros((128, 128), f32)
     for p in range(3):
-        block = jnp.where(kind == p, density[:, p * 128 : p * 128 + 128], block)
-    high = block.astype(bf16)
-    out[:, 512:640] = high
-    out[:, 640:768] = (block - high.astype(f32)).astype(bf16)
+        lanes = slice(p * 128, p * 128 + 128)
+        block = jnp.where(kind == p, high[:, lanes], block)
+        block = jnp.where(kind == 3 + p, density[:, lanes] - high[:, lanes], block)
+    out[:, 512:640] = block.astype(bf16)
 
 
 def sum_kernel(parts, rows, density):
-    row = lax.broadcasted_iota(jnp.int32, (4 * SLABS, 128), 0)
-    col = lax.broadcasted_iota(jnp.int32, (4 * SLABS, 128), 1)
-    adder = jnp.where((row & 3) == (col & 3), 1.0, 0.0).astype(bf16)
-    rows[...] = product(adder, parts[:, 0:512])
+    row = lax.broadcasted_iota(jnp.int32, (16, 128), 0)
+    col = lax.broadcasted_iota(jnp.int32, (16, 128), 1)
+    adder = jnp.where(row == (col & 15), 1.0, 0.0).astype(bf16)
+    total = product(adder, parts[:, 0:512]).astype(bf16)
+    for receiver in range(SLABS):
+        rows[receiver * 16 : receiver * 16 + 16] = total
     row = lax.broadcasted_iota(jnp.int32, (8, 128), 0)
     col = lax.broadcasted_iota(jnp.int32, (8, 128), 1)
     half = jnp.where(row >= 3, 1, 0)
     for lane_block in range(4):
-        sender = lane_block * 8 + 2 * lax.axis_index("x") + half
-        pick = jnp.where((col == sender * 4 + row - 3 * half) & (row < THICK), 1.0, 0.0).astype(bf16)
+        first = (lane_block * 2 + half) * 16 + row - 3 * half
+        hit = ((col == first) | (col == first + 3)) & (row < THICK)
+        pick = jnp.where(hit, 1.0, 0.0).astype(bf16)
         lanes = slice(lane_block * 128, lane_block * 128 + 128)
-        density[:, lanes] = product(pick, parts[:, 512:640]) + product(pick, parts[:, 640:768])
+        density[:, lanes] = product(pick, parts[:, 512:640])
 
 
 def final_kernel(rows, cells, energy, gram, density):
-    scale = 1.0 / (NZ * PLANE)
-    for x in range(4):
-        total = rows[12 * x : 12 * x + 4] + rows[12 * x + 4 : 12 * x + 8] + rows[12 * x + 8 : 12 * x + 12]
-        total = total * scale
-        energy[2 * x : 2 * x + 2] = total[0:2]
-        gram[2 * x : 2 * x + 2] = total[2:4]
+    total = rows[0:16].astype(f32)
+    for sender in range(1, SLABS):
+        total = total + rows[sender * 16 : sender * 16 + 16].astype(f32)
+    total = total * (1.0 / (NZ * PLANE))
+    energy[...] = total[0:8]
+    gram[...] = total[8:16]
     for line in range(NX):
         density[:, line, :] = cells[0:THICK, line * NY : line * NY + NY]
 
@@ -202,31 +211,32 @@
     send = pl.pallas_call(
         filter_kernel,
         out_shape=jax.ShapeDtypeStruct((64, 896), bf16),
-        in_specs=[vmem] * 7,
+        in_specs=[pl.BlockSpec(memory_space=pltpu.HBM)] + [vmem] * 6,
         out_specs=vmem,
+        scratch_shapes=[pltpu.VMEM((1, 8), f32), pltpu.SemaphoreType.DMA(())],
         compiler_params=params,
         name="chebyshev",
     )(occupation.reshape(1, 8), slabs, unpack, plane_high, plane_low, depth_high, depth_low)
 
-    own = exchange(send.reshape(32, 2, 896), ("zl", "y")).reshape(64, 896)
+    own = exchange(send.reshape(32, 2, 896), ("y", "x")).reshape(64, 896)
     shared = jnp.broadcast_to(own[None, :, :512], (4, 64, 512))
-    gathered = exchange(shared, "x").reshape(256, 512)
+    gathered = exchange(shared, "zl").reshape(256, 512)
     gathered = lax.all_gather(gathered, "c", axis=0, tiled=True)
 
     partial = pl.pallas_call(
         tile_kernel,
-        out_shape=jax.ShapeDtypeStruct((128, 768), bf16),
+        out_shape=jax.ShapeDtypeStruct((128, 640), bf16),
         in_specs=[vmem] * 2,
         out_specs=vmem,
         compiler_params=params,
         name="tiles",
     )(own, gathered)
 
-    parts = exchange(partial.reshape(32, 4, 768), ("zl", "y")).reshape(128, 768)
+    parts = exchange(partial.reshape(8, 16, 640), "y").reshape(128, 640)
     rows, cells = pl.pallas_call(
         sum_kernel,
         out_shape=[
-            jax.ShapeDtypeStruct((4 * SLABS, NS), f32),
+            jax.ShapeDtypeStruct((16 * SLABS, NS), bf16),
             jax.ShapeDtypeStruct((8, PLANE), f32),
         ],
         in_specs=[vmem],
@@ -235,7 +245,7 @@
         name="sums",
     )(parts)
 
-    rows = exchange(rows.reshape(SLABS, 4, NS), ("x", "zh")).reshape(4 * SLABS, NS)
+    rows = exchange(rows.reshape(SLABS, 16, NS), ("x", "zh")).reshape(16 * SLABS, NS)
     return pl.pallas_call(
         final_kernel,
         out_shape=[

time: 103 us -> 104 us (level)
  the two profiles are of different devices: /device:TPU:8 before, /device:TPU:1 now
where the time goes in v4:
time: 104 us; the launch traced here: 103 us
  blocking collectives  96.6 us (93%)
  Pallas kernels  3.86 us (4%)
  local copies, waits for them, and re-layouts  1.1 us (1%)
    all_to_all x5, blocking collectives, exchange(): return lax.all_to_all(array, axes, 0, 0, tiled=True)  90.9 us
    all_gather x1, blocking collectives, body(): gathered = lax.all_gather(gathered, 'c', axis=0, tiled=True)  5.73 us
    pallas_call x1, Pallas kernels, body(): pl.pallas_call(filter_kernel, out_shape=jax.ShapeDtypeStruct((64, 896), b...  2.25 us

profile of v4, /device:TPU:1, one launch (start us, length us, event | category | flops | bytes accessed | tf_op | source)
XLA Modules:
  0.0 103.3 jit_solution(1486137780793029237)
XLA Ops:
  0.6 0.0 copy-start.6
  0.6 0.8 fusion.2
  1.5 0.1 broadcast_in_dim.8
  1.6 0.0 copy-done.6
  1.6 0.0 copy-start.3
  1.6 0.0 copy-start.4
  1.7 0.2 reshape.44
  1.8 0.0 copy-start.2
  1.9 0.0 copy-start.1
  1.9 0.0 copy-start
  2.0 28.7 %all_to_all.25 = bf16[12,24,512]{2,1,0:T(8,128)(2,1)S(1)} all-to-all(bf16[12,24,512]{2,1,0:T(8,128)(2,1)S(1)} %bitcast.22), channel_id=1, replica_groups=mesh['x'=4,'zh'=3,'zl'=4,'y'=8,'c'=2] {'x','zh'}, dimensions={0} | all-to-all | bytes 589824 | tf_op jit(solution)/shard_map/all_to_all | solution.py:195
  30.7 0.0 copy-start.5
  30.7 0.0 copy-done.3
  30.7 0.0 copy-done.4
  30.7 0.0 copy-done.2
  30.7 0.0 copy-done.1
  30.7 0.0 copy-done
  30.7 0.6 copy-done.5
  31.4 2.2 %chebyshev.1 = bf16[64,896]{1,0:T(8,128)(2,1)S(1)} custom-call(f32[1,8]{1,0:T(1,128)S(1)} %bitcast.21, bf16[288,512]{1,0:T(8,128)(2,1)S(1)} %bitcast.16, bf16[288,288]{1,0:T(8,128)(2,1)S(1)} %copy-done.2, bf16[512,512]{1,0:T(8,128)(2,1)S(1)} %copy-done.1, bf16[512,512]{1,0:T(8,128)(2,1)S(1)} %copy-done, bf16[144,144]{1,0:T(8,128)(2,1)S(1)} %copy-done.4, ...), custom_call_target="tpu_custom_call" | custom-call | tf_op jit(solution)/shard_map/chebyshev/pallas_call | solution.py:211
  33.7 16.8 %all_to_all.26 = bf16[32,2,896]{2,1,0:T(2,128)(2,1)S(1)} all-to-all(bf16[32,2,896]{2,1,0:T(2,128)(2,1)S(1)} %reshape.47), channel_id=1, replica_groups=mesh['x'=4,'zh'=3,'zl'=4,'y'=8,'c'=2] {'y','x'}, dimensions={0} | all-to-all | bytes 229376 | tf_op jit(solution)/shard_map/all_to_all | solution.py:195
  50.6 15.8 %all_to_all.27 = bf16[4,64,512]{2,1,0:T(8,128)(2,1)S(1)} all-to-all(bf16[4,64,512]{2,1,0:T(8,128)(2,1)S(1)} %broadcast_in_dim.22), channel_id=1, replica_groups=mesh['x'=4,'zh'=3,'zl'=4,'y'=8,'c'=2] {'zl'}, dimensions={0} | all-to-all | bytes 524288 | tf_op jit(solution)/shard_map/all_to_all | solution.py:195
  66.4 5.7 %all_gather.3.gathered = bf16[512,512]{1,0:T(8,128)(2,1)S(1)} all-gather(bf16[256,512]{1,0:T(8,128)(2,1)S(1)} %bitcast.23), channel_id=1, replica_groups=mesh['x'=4,'zh'=3,'zl'=4,'y'=8,'c'=2] {'c'}, dimensions={0}, use_global_device_ids=true | all-gather | bytes 786432 | tf_op jit(solution)/shard_map/all_gather | solution.py:224
  72.1 0.7 tiles.1
  72.8 11.5 %all_to_all.28 = bf16[8,16,640]{2,1,0:T(8,128)(2,1)S(1)} all-to-all(bf16[8,16,640]{2,1,0:T(8,128)(2,1)S(1)} %bitcast.19), channel_id=1, replica_groups=mesh['x'=4,'zh'=3,'zl'=4,'y'=8,'c'=2] {'y'}, dimensions={0} | all-to-all | bytes 327680 | tf_op jit(solution)/shard_map/all_to_all | solution.py:195
  84.3 0.2 sums.1
  84.5 18.0 %all_to_all.29 = bf16[12,16,512]{2,1,0:T(8,128)(2,1)S(1)} all-to-all(bf16[12,16,512]{2,1,0:T(8,128)(2,1)S(1)} %bitcast.20), channel_id=1, replica_groups=mesh['x'=4,'zh'=3,'zl'=4,'y'=8,'c'=2] {'x','zh'}, dimensions={0} | all-to-all | bytes 393216 | tf_op jit(solution)/shard_map/all_to_all | solution.py:195
  102.5 0.8 results.1
  (8 shorter events, 0.2 us)
Async XLA Ops:
  0.6 1.0 copy-start.6
  1.6 29.1 %copy-start.3 = (bf16[144,144]{1,0:T(8,128)(2,1)S(1)}, bf16[144,144]{1,0:T(8,128)(2,1)}, u32[]{:S(2)}) copy-start(bf16[144,144]{1,0:T(8,128)(2,1)} %constant.14.clone.low_z) | copy-start | bytes 124420
  1.6 29.1 %copy-start.4 = (bf16[144,144]{1,0:T(8,128)(2,1)S(1)}, bf16[144,144]{1,0:T(8,128)(2,1)}, u32[]{:S(2)}) copy-start(bf16[144,144]{1,0:T(8,128)(2,1)} %constant.13.clone.high_z) | copy-start | bytes 124420
  1.8 28.9 %copy-start.2 = (bf16[288,288]{1,0:T(8,128)(2,1)S(1)}, bf16[288,288]{1,0:T(8,128)(2,1)}, u32[]{:S(2)}) copy-start(bf16[288,288]{1,0:T(8,128)(2,1)} %constant.10.clone.unpack_rows) | copy-start | bytes 497668
  1.9 28.9 %copy-start.1 = (bf16[512,512]{1,0:T(8,128)(2,1)S(1)}, bf16[512,512]{1,0:T(8,128)(2,1)}, u32[]{:S(2)}) copy-start(bf16[512,512]{1,0:T(8,128)(2,1)} %constant.11.clone.high_xy) | copy-start | bytes 1572868
  1.9 28.8 %copy-start = (bf16[512,512]{1,0:T(8,128)(2,1)S(1)}, bf16[512,512]{1,0:T(8,128)(2,1)}, u32[]{:S(2)}) copy-start(bf16[512,512]{1,0:T(8,128)(2,1)} %constant.12.clone.low_xy) | copy-start | bytes 1572868
  30.7 0.7 copy-start.5

commit v5 on v3

--- a/solution.py
+++ b/solution.py
@@ -160,7 +160,7 @@
     row = lax.broadcasted_iota(jnp.int32, (4 * SLABS, 128), 0)
     col = lax.broadcasted_iota(jnp.int32, (4 * SLABS, 128), 1)
     adder = jnp.where((row & 3) == (col & 3), 1.0, 0.0).astype(bf16)
-    rows[...] = product(adder, parts[:, 0:512])
+    rows[...] = product(adder, parts[:, 0:512]).astype(bf16)
     row = lax.broadcasted_iota(jnp.int32, (8, 128), 0)
     col = lax.broadcasted_iota(jnp.int32, (8, 128), 1)
     half = jnp.where(row >= 3, 1, 0)
@@ -171,7 +171,8 @@
         density[:, lanes] = product(pick, parts[:, 512:640]) + product(pick, parts[:, 640:768])
 
 
-def final_kernel(rows, cells, energy, gram, density):
+def final_kernel(received, cells, energy, gram, density):
+    rows = received[...].astype(f32)
     scale = 1.0 / (NZ * PLANE)
     for x in range(4):
         total = rows[12 * x : 12 * x + 4] + rows[12 * x + 4 : 12 * x + 8] + rows[12 * x + 8 : 12 * x + 12]
@@ -226,7 +227,7 @@
     rows, cells = pl.pallas_call(
         sum_kernel,
         out_shape=[
-            jax.ShapeDtypeStruct((4 * SLABS, NS), f32),
+            jax.ShapeDtypeStruct((4 * SLABS, NS), bf16),
             jax.ShapeDtypeStruct((8, PLANE), f32),
         ],
         in_specs=[vmem],

time: 103 us -> 101 us (0.981)
  blocking collectives: 95.4 us -> 94 us
    all_to_all x5, blocking collectives: 93.3 us -> 91.8 us  [exchange(): return lax.all_to_all(array, axes, 0, 0, tiled=True)]
where the time goes in v5:
time: 101 us
  blocking collectives  94 us (93%)
  Pallas kernels  3.82 us (4%)
  local copies, waits for them, and re-layouts  1.24 us (1%)
    all_to_all x5, blocking collectives, exchange(): return lax.all_to_all(array, axes, 0, 0, tiled=True)  91.8 us
    all_gather x1, blocking collectives, body(): gathered = lax.all_gather(gathered, 'c', axis=0, tiled=True)  2.17 us
    pallas_call x1, Pallas kernels, body(): pl.pallas_call(filter_kernel, out_shape=jax.ShapeDtypeStruct((64, 896), b...  2.15 us

profile of v5, /device:TPU:8, one launch (start us, length us, event | category | flops | bytes accessed | tf_op | source)
XLA Modules:
  0.0 100.7 jit_solution(165398008734740764)
XLA Ops:
  0.6 0.0 copy-start.6
  0.6 0.8 fusion.2
  1.5 0.1 broadcast_in_dim.8
  1.6 0.0 copy-done.6
  1.6 0.0 copy-start.3
  1.6 0.0 copy-start.4
  1.7 0.2 reshape.44
  1.8 0.0 copy-start.2
  1.9 0.0 copy-start.1
  1.9 0.0 copy-start
  2.0 32.8 %all_to_all.25 = bf16[12,24,512]{2,1,0:T(8,128)(2,1)S(1)} all-to-all(bf16[12,24,512]{2,1,0:T(8,128)(2,1)S(1)} %bitcast.14), channel_id=1, replica_groups=mesh['x'=4,'zh'=3,'zl'=4,'y'=8,'c'=2] {'x','zh'}, dimensions={0} | all-to-all | bytes 589824 | tf_op jit(solution)/shard_map/all_to_all | solution.py:187
  34.7 0.0 copy-start.5
  34.7 0.0 copy-done.3
  34.7 0.0 copy-done.4
  34.7 0.0 copy-done.2
  34.7 0.0 copy-done.1
  34.7 0.0 copy-done
  34.7 0.6 copy-done.5
  35.4 2.1 %chebyshev.1 = bf16[64,896]{1,0:T(8,128)(2,1)S(1)} custom-call(f32[1,8]{1,0:T(1,128)S(1)} %bitcast.13, bf16[288,512]{1,0:T(8,128)(2,1)S(1)} %bitcast.12, bf16[288,288]{1,0:T(8,128)(2,1)S(1)} %copy-done.2, bf16[512,512]{1,0:T(8,128)(2,1)S(1)} %copy-done.1, bf16[512,512]{1,0:T(8,128)(2,1)S(1)} %copy-done, bf16[144,144]{1,0:T(8,128)(2,1)S(1)} %copy-done.4, ...), custom_call_target="tpu_custom_call" | custom-call | tf_op jit(solution)/shard_map/chebyshev/pallas_call | solution.py:203
  37.6 20.6 %all_to_all.26 = bf16[32,2,896]{2,1,0:T(2,128)(2,1)S(1)} all-to-all(bf16[32,2,896]{2,1,0:T(2,128)(2,1)S(1)} %reshape.47), channel_id=1, replica_groups=mesh['x'=4,'zh'=3,'zl'=4,'y'=8,'c'=2] {'zl','y'}, dimensions={0} | all-to-all | bytes 229376 | tf_op jit(solution)/shard_map/all_to_all | solution.py:187
  58.3 9.1 %all_to_all.27 = bf16[4,64,512]{2,1,0:T(8,128)(2,1)S(1)} all-to-all(bf16[4,64,512]{2,1,0:T(8,128)(2,1)S(1)} %broadcast_in_dim.22), channel_id=1, replica_groups=mesh['x'=4,'zh'=3,'zl'=4,'y'=8,'c'=2] {'x'}, dimensions={0} | all-to-all | bytes 524288 | tf_op jit(solution)/shard_map/all_to_all | solution.py:187
  67.4 2.2 %all_gather.3.gathered = bf16[512,512]{1,0:T(8,128)(2,1)S(1)} all-gather(bf16[256,512]{1,0:T(8,128)(2,1)S(1)} %bitcast.15), channel_id=1, replica_groups=mesh['x'=4,'zh'=3,'zl'=4,'y'=8,'c'=2] {'c'}, dimensions={0}, use_global_device_ids=true | all-gather | bytes 786432 | tf_op jit(solution)/shard_map/all_gather | solution.py:215
  69.6 0.7 tiles.1
  70.3 0.1 reshape.50
  70.3 14.9 %all_to_all.28 = bf16[32,4,768]{2,1,0:T(4,128)(2,1)S(1)} all-to-all(bf16[32,4,768]{2,1,0:T(4,128)(2,1)S(1)} %reshape.50), channel_id=1, replica_groups=mesh['x'=4,'zh'=3,'zl'=4,'y'=8,'c'=2] {'zl','y'}, dimensions={0} | all-to-all | bytes 393216 | tf_op jit(solution)/shard_map/all_to_all | solution.py:187
  85.2 0.1 reshape.51.parts
  85.2 0.2 sums.1
  85.4 14.5 %all_to_all.29 = bf16[12,4,512]{2,1,0:T(4,128)(2,1)S(1)} all-to-all(bf16[12,4,512]{2,1,0:T(4,128)(2,1)S(1)} %reshape.52), channel_id=1, replica_groups=mesh['x'=4,'zh'=3,'zl'=4,'y'=8,'c'=2] {'x','zh'}, dimensions={0} | all-to-all | bytes 98304 | tf_op jit(solution)/shard_map/all_to_all | solution.py:187
  100.0 0.8 results.1
  (10 shorter events, 0.2 us)
Async XLA Ops:
  0.6 1.0 copy-start.6
  1.6 33.1 %copy-start.3 = (bf16[144,144]{1,0:T(8,128)(2,1)S(1)}, bf16[144,144]{1,0:T(8,128)(2,1)}, u32[]{:S(2)}) copy-start(bf16[144,144]{1,0:T(8,128)(2,1)} %constant.14.clone.low_z) | copy-start | bytes 124420
  1.6 33.1 %copy-start.4 = (bf16[144,144]{1,0:T(8,128)(2,1)S(1)}, bf16[144,144]{1,0:T(8,128)(2,1)}, u32[]{:S(2)}) copy-start(bf16[144,144]{1,0:T(8,128)(2,1)} %constant.13.clone.high_z) | copy-start | bytes 124420
  1.8 32.9 %copy-start.2 = (bf16[288,288]{1,0:T(8,128)(2,1)S(1)}, bf16[288,288]{1,0:T(8,128)(2,1)}, u32[]{:S(2)}) copy-start(bf16[288,288]{1,0:T(8,128)(2,1)} %constant.10.clone.unpack_rows) | copy-start | bytes 497668
  1.9 32.9 %copy-start.1 = (bf16[512,512]{1,0:T(8,128)(2,1)S(1)}, bf16[512,512]{1,0:T(8,128)(2,1)}, u32[]{:S(2)}) copy-start(bf16[512,512]{1,0:T(8,128)(2,1)} %constant.11.clone.high_xy) | copy-start | bytes 1572868
  1.9 32.8 %copy-start = (bf16[512,512]{1,0:T(8,128)(2,1)S(1)}, bf16[512,512]{1,0:T(8,128)(2,1)}, u32[]{:S(2)}) copy-start(bf16[512,512]{1,0:T(8,128)(2,1)} %constant.12.clone.low_xy) | copy-start | bytes 1572868
  34.7 0.7 copy-start.5

commit v6 on v5

--- a/solution.py
+++ b/solution.py
@@ -1,3 +1,5 @@
+import math
+
 import jax
 import jax.numpy as jnp
 import numpy as np
@@ -30,6 +32,8 @@
 cut_high = 12.0
 centre = 0.5 * (cut_high + cut_low)
 spread = 0.5 * (cut_high - cut_low)
+CODE = 120.0
+OFFSET = 0.5
 bf16 = jnp.bfloat16
 f32 = jnp.float32
 
@@ -56,15 +60,19 @@
 
 
 def unpacking():
-    matrix = np.zeros((4 * NZ, 4 * NZ), np.float32)
+    matrix = np.zeros((9 * NZ, SLABS * 8), np.float32)
     for slab in range(SLABS):
         for plane in range(THICK):
+            z = slab * THICK + plane
             for state in range(2):
-                z = slab * THICK + plane
-                base = slab * 4 * THICK + plane
-                matrix[state * NZ + z, base + state * THICK] = 1.0
-                matrix[(2 + state) * NZ + z, base + 2 * THICK] = 1.0
-                matrix[(2 + state) * NZ + z, base + 3 * THICK] = 1.0
+                line = state * THICK + plane
+                start = 0 if line < 8 else 6 * NZ
+                matrix[start + state * NZ + z, slab * 8 + line % 8] = 1.0
+            if plane < 4:
+                matrix[8 * NZ + z, slab * 8 + 4 + plane] = 1.0
+            else:
+                for block in range(4):
+                    matrix[(2 + block) * NZ + z, slab * 8 + (plane - 4) * 4 + block] = 1.0
     return matrix.astype(bf16)
 
 
@@ -77,9 +85,14 @@
 
 def filter_kernel(occupation, slabs, unpack_rows, high_xy, low_xy, high_z, low_z, out):
     count = 2 * NZ
-    everything = product(unpack_rows[...], slabs[...])
-    first = everything[:count]
-    diagonal = everything[count:] - 1.5 * stencil_weights[0]
+    left, middle, right = slabs[:, 0:512], slabs[:, 512:1024], slabs[:, 1024:1152]
+    first = product(unpack_rows[0:count], left) + product(unpack_rows[6 * NZ : 8 * NZ], middle)
+    pieces = product(unpack_rows[count : 6 * NZ], right)
+    code = product(unpack_rows[8 * NZ : 9 * NZ], middle) + jnp.concatenate(
+        [pieces[block * NZ : block * NZ + NZ] for block in range(4)], axis=1
+    )
+    levels = jnp.log(code) * (1.0 / (CODE * math.log(2.0))) - OFFSET - 1.5 * stencil_weights[0]
+    diagonal = jnp.concatenate([levels, levels], axis=0)
     shifted = diagonal - centre
 
     def hop(v):
@@ -188,15 +201,15 @@
 
 
 def body(orbitals, potential, occupation):
-    high = lax.reduce_precision(potential, 8, 7)
-    low = potential - high
-    wells = jnp.stack([high.astype(bf16), low.astype(bf16)]).reshape(1, 2 * THICK, PLANE)
-    slabs = jnp.concatenate(
-        [orbitals.reshape(4, 2 * THICK, PLANE), jnp.broadcast_to(wells, (4, 2 * THICK, PLANE))],
-        axis=1,
-    )
-    slabs = jnp.broadcast_to(slabs[:, None], (4, 3, 4 * THICK, PLANE)).reshape(SLABS, 4 * THICK, PLANE)
-    slabs = exchange(slabs, ("x", "zh")).reshape(4 * NZ, PLANE)
+    code = jnp.exp2(CODE * (potential + OFFSET)).astype(bf16)
+    wells = jnp.stack([code, code]).reshape(1, 2 * THICK, PLANE)
+    rows = jnp.concatenate(
+        [orbitals.reshape(4, 2 * THICK, PLANE), jnp.broadcast_to(wells, (4, 2 * THICK, PLANE))], axis=1
+    )
+    rest = rows[:, 16:18].reshape(4, 8, 128)
+    slabs = jnp.concatenate([rows[:, :8], rows[:, 8:16], rest], axis=2)
+    slabs = jnp.broadcast_to(slabs[:, None], (4, 3, 8, 1152)).reshape(SLABS, 8, 1152)
+    slabs = exchange(slabs, ("x", "zh")).reshape(SLABS * 8, 1152)
 
     vmem = pl.BlockSpec(memory_space=pltpu.VMEM)
     params = pltpu.CompilerParams(vmem_limit_bytes=24 * 1024 * 1024)

time: 101 us -> 99 us (0.980)
  blocking collectives: 94 us -> 91.9 us
    all_to_all x5, blocking collectives: 91.8 us -> 89.7 us  [exchange(): return lax.all_to_all(array, axes, 0, 0, tiled=True)]
where the time goes in v6:
time: 99 us; the launch traced here: 98.6 us
  blocking collectives  91.9 us (93%)
  Pallas kernels  3.79 us (4%)
  local copies, waits for them, and re-layouts  1.27 us (1%)
    all_to_all x5, blocking collectives, exchange(): return lax.all_to_all(array, axes, 0, 0, tiled=True)  89.7 us
    all_gather x1, blocking collectives, body(): gathered = lax.all_gather(gathered, 'c', axis=0, tiled=True)  2.17 us
    pallas_call x1, Pallas kernels, body(): pl.pallas_call(filter_kernel, out_shape=jax.ShapeDtypeStruct((64, 896), b...  2.12 us

profile of v6, /device:TPU:8, one launch (start us, length us, event | category | flops | bytes accessed | tf_op | source)
XLA Modules:
  0.0 98.6 jit_solution(12128059818748647603)
XLA Ops:
  0.6 0.0 copy-start.6
  0.6 0.9 fusion.2
  1.5 0.1 broadcast_in_dim.23
  1.7 0.0 copy-done.6
  1.7 0.0 copy-start.2
  1.7 0.0 copy-start.4
  1.7 0.2 reshape.46
  1.9 0.0 copy-start.3
  1.9 0.0 copy-start
  1.9 0.0 copy-start.1
  2.0 28.3 %all_to_all.25 = bf16[12,8,1152]{2,1,0:T(8,128)(2,1)S(1)} all-to-all(bf16[12,8,1152]{2,1,0:T(8,128)(2,1)S(1)} %bitcast.13), channel_id=1, replica_groups=mesh['x'=4,'zh'=3,'zl'=4,'y'=8,'c'=2] {'x','zh'}, dimensions={0} | all-to-all | bytes 442368 | tf_op jit(solution)/shard_map/all_to_all | solution.py:200
  30.3 0.0 copy-start.5
  30.3 0.0 copy-done.2
  30.3 0.0 copy-done.4
  30.3 0.0 copy-done.3
  30.3 0.0 copy-done
  30.3 0.0 copy-done.1
  30.3 0.6 copy-done.5
  30.9 2.1 %chebyshev.1 = bf16[64,896]{1,0:T(8,128)(2,1)S(1)} custom-call(f32[1,8]{1,0:T(1,128)S(1)} %bitcast.11, bf16[96,1152]{1,0:T(8,128)(2,1)S(1)} %bitcast.10, bf16[648,96]{1,0:T(8,128)(2,1)S(1)} %copy-done.2, bf16[512,512]{1,0:T(8,128)(2,1)S(1)} %copy-done.1, bf16[512,512]{1,0:T(8,128)(2,1)S(1)} %copy-done, bf16[144,144]{1,0:T(8,128)(2,1)S(1)} %copy-done.4, ...), custom_call_target="tpu_custom_call" | custom-call | tf_op jit(solution)/shard_map/chebyshev/pallas_call | solution.py:216
  33.1 0.1 reshape.49
  33.1 22.8 %all_to_all.26 = bf16[32,2,896]{2,1,0:T(2,128)(2,1)S(1)} all-to-all(bf16[32,2,896]{2,1,0:T(2,128)(2,1)S(1)} %reshape.49), channel_id=1, replica_groups=mesh['x'=4,'zh'=3,'zl'=4,'y'=8,'c'=2] {'zl','y'}, dimensions={0} | all-to-all | bytes 229376 | tf_op jit(solution)/shard_map/all_to_all | solution.py:200
  56.0 9.1 %all_to_all.27 = bf16[4,64,512]{2,1,0:T(8,128)(2,1)S(1)} all-to-all(bf16[4,64,512]{2,1,0:T(8,128)(2,1)S(1)} %broadcast_in_dim.28), channel_id=1, replica_groups=mesh['x'=4,'zh'=3,'zl'=4,'y'=8,'c'=2] {'x'}, dimensions={0} | all-to-all | bytes 524288 | tf_op jit(solution)/shard_map/all_to_all | solution.py:200
  65.1 2.2 %all_gather.3.gathered = bf16[512,512]{1,0:T(8,128)(2,1)S(1)} all-gather(bf16[256,512]{1,0:T(8,128)(2,1)S(1)} %bitcast.12), channel_id=1, replica_groups=mesh['x'=4,'zh'=3,'zl'=4,'y'=8,'c'=2] {'c'}, dimensions={0}, use_global_device_ids=true | all-gather | bytes 786432 | tf_op jit(solution)/shard_map/all_gather | solution.py:228
  67.3 0.7 tiles.1
  68.0 0.1 reshape.52
  68.0 14.9 %all_to_all.28 = bf16[32,4,768]{2,1,0:T(4,128)(2,1)S(1)} all-to-all(bf16[32,4,768]{2,1,0:T(4,128)(2,1)S(1)} %reshape.52), channel_id=1, replica_groups=mesh['x'=4,'zh'=3,'zl'=4,'y'=8,'c'=2] {'zl','y'}, dimensions={0} | all-to-all | bytes 393216 | tf_op jit(solution)/shard_map/all_to_all | solution.py:200
  82.9 0.1 reshape.53.parts
  82.9 0.2 sums.1
  83.2 14.7 %all_to_all.29 = bf16[12,4,512]{2,1,0:T(4,128)(2,1)S(1)} all-to-all(bf16[12,4,512]{2,1,0:T(4,128)(2,1)S(1)} %reshape.54), channel_id=1, replica_groups=mesh['x'=4,'zh'=3,'zl'=4,'y'=8,'c'=2] {'x','zh'}, dimensions={0} | all-to-all | bytes 98304 | tf_op jit(solution)/shard_map/all_to_all | solution.py:200
  97.9 0.8 results.1
  (13 shorter events, 0.2 us)
Async XLA Ops:
  0.6 1.0 %copy-start.6 = (bf16[8,6,16,32]{3,2,1,0:T(8,128)(2,1)S(1)}, bf16[8,6,16,32]{3,2,1,0:T(8,128)(2,1)}, u32[]{:S(2)}) copy-start(bf16[8,6,16,32]{3,2,1,0:T(8,128)(2,1)} %param.8) | copy-start | bytes 147460
  1.7 28.6 %copy-start.2 = (bf16[648,96]{1,0:T(8,128)(2,1)S(1)}, bf16[648,96]{1,0:T(8,128)(2,1)}, u32[]{:S(2)}) copy-start(bf16[648,96]{1,0:T(8,128)(2,1)} %constant.16.clone.unpack_rows) | copy-start | bytes 373252
  1.7 28.6 %copy-start.4 = (bf16[144,144]{1,0:T(8,128)(2,1)S(1)}, bf16[144,144]{1,0:T(8,128)(2,1)}, u32[]{:S(2)}) copy-start(bf16[144,144]{1,0:T(8,128)(2,1)} %constant.19.clone.high_z) | copy-start | bytes 124420
  1.9 28.4 %copy-start.3 = (bf16[144,144]{1,0:T(8,128)(2,1)S(1)}, bf16[144,144]{1,0:T(8,128)(2,1)}, u32[]{:S(2)}) copy-start(bf16[144,144]{1,0:T(8,128)(2,1)} %constant.20.clone.low_z) | copy-start | bytes 124420
  1.9 28.4 %copy-start = (bf16[512,512]{1,0:T(8,128)(2,1)S(1)}, bf16[512,512]{1,0:T(8,128)(2,1)}, u32[]{:S(2)}) copy-start(bf16[512,512]{1,0:T(8,128)(2,1)} %constant.18.clone.low_xy) | copy-start | bytes 1572868
  1.9 28.4 %copy-start.1 = (bf16[512,512]{1,0:T(8,128)(2,1)S(1)}, bf16[512,512]{1,0:T(8,128)(2,1)}, u32[]{:S(2)}) copy-start(bf16[512,512]{1,0:T(8,128)(2,1)} %constant.17.clone.high_xy) | copy-start | bytes 1572868
  30.3 0.7 copy-start.5

commit v7 on v6

--- a/solution.py
+++ b/solution.py
@@ -18,6 +18,7 @@
 PLANE = NX * NY
 SLABS = 12
 THICK = NZ // SLABS
+PICKED = 9 * NZ + 8
 
 stencil_weights = (
     -5369.0 / 1800.0,
@@ -60,7 +61,7 @@
 
 
 def unpacking():
-    matrix = np.zeros((9 * NZ, SLABS * 8), np.float32)
+    matrix = np.zeros((PICKED, SLABS * 8), np.float32)
     for slab in range(SLABS):
         for plane in range(THICK):
             z = slab * THICK + plane
@@ -88,7 +89,7 @@
     left, middle, right = slabs[:, 0:512], slabs[:, 512:1024], slabs[:, 1024:1152]
     first = product(unpack_rows[0:count], left) + product(unpack_rows[6 * NZ : 8 * NZ], middle)
     pieces = product(unpack_rows[count : 6 * NZ], right)
-    code = product(unpack_rows[8 * NZ : 9 * NZ], middle) + jnp.concatenate(
+    code = product(unpack_rows[8 * NZ : PICKED], middle)[:NZ] + jnp.concatenate(
         [pieces[block * NZ : block * NZ + NZ] for block in range(4)], axis=1
     )
     levels = jnp.log(code) * (1.0 / (CODE * math.log(2.0))) - OFFSET - 1.5 * stencil_weights[0]

time: 99 us -> 99 us (level)
  no operation moved by 1% of the time
where the time goes in v7:
time: 99 us; the launch traced here: 98.6 us
  blocking collectives  91.9 us (93%)
  Pallas kernels  3.79 us (4%)
  local copies, waits for them, and re-layouts  1.27 us (1%)
    all_to_all x5, blocking collectives, exchange(): return lax.all_to_all(array, axes, 0, 0, tiled=True)  89.7 us
    all_gather x1, blocking collectives, body(): gathered = lax.all_gather(gathered, 'c', axis=0, tiled=True)  2.17 us
    pallas_call x1, Pallas kernels, body(): pl.pallas_call(filter_kernel, out_shape=jax.ShapeDtypeStruct((64, 896), b...  2.12 us

profile of v7, /device:TPU:8, one launch (start us, length us, event | category | flops | bytes accessed | tf_op | source)
XLA Modules:
  0.0 98.6 jit_solution(8873474862149740364)
XLA Ops:
  0.6 0.0 copy-start.6
  0.6 0.9 fusion.2
  1.5 0.1 broadcast_in_dim.23
  1.7 0.0 copy-done.6
  1.7 0.0 copy-start.2
  1.7 0.0 copy-start.4
  1.7 0.2 reshape.46
  1.9 0.0 copy-start.3
  1.9 0.0 copy-start
  1.9 0.0 copy-start.1
  2.0 28.3 %all_to_all.25 = bf16[12,8,1152]{2,1,0:T(8,128)(2,1)S(1)} all-to-all(bf16[12,8,1152]{2,1,0:T(8,128)(2,1)S(1)} %bitcast.13), channel_id=1, replica_groups=mesh['x'=4,'zh'=3,'zl'=4,'y'=8,'c'=2] {'x','zh'}, dimensions={0} | all-to-all | bytes 442368 | tf_op jit(solution)/shard_map/all_to_all | solution.py:201
  30.3 0.0 copy-start.5
  30.3 0.0 copy-done.2
  30.3 0.0 copy-done.4
  30.3 0.0 copy-done.3
  30.3 0.0 copy-done
  30.3 0.0 copy-done.1
  30.3 0.6 copy-done.5
  30.9 2.1 %chebyshev.1 = bf16[64,896]{1,0:T(8,128)(2,1)S(1)} custom-call(f32[1,8]{1,0:T(1,128)S(1)} %bitcast.11, bf16[96,1152]{1,0:T(8,128)(2,1)S(1)} %bitcast.10, bf16[656,96]{1,0:T(8,128)(2,1)S(1)} %copy-done.2, bf16[512,512]{1,0:T(8,128)(2,1)S(1)} %copy-done.1, bf16[512,512]{1,0:T(8,128)(2,1)S(1)} %copy-done, bf16[144,144]{1,0:T(8,128)(2,1)S(1)} %copy-done.4, ...), custom_call_target="tpu_custom_call" | custom-call | tf_op jit(solution)/shard_map/chebyshev/pallas_call | solution.py:217
  33.1 0.1 reshape.49
  33.1 22.8 %all_to_all.26 = bf16[32,2,896]{2,1,0:T(2,128)(2,1)S(1)} all-to-all(bf16[32,2,896]{2,1,0:T(2,128)(2,1)S(1)} %reshape.49), channel_id=1, replica_groups=mesh['x'=4,'zh'=3,'zl'=4,'y'=8,'c'=2] {'zl','y'}, dimensions={0} | all-to-all | bytes 229376 | tf_op jit(solution)/shard_map/all_to_all | solution.py:201
  56.0 9.1 %all_to_all.27 = bf16[4,64,512]{2,1,0:T(8,128)(2,1)S(1)} all-to-all(bf16[4,64,512]{2,1,0:T(8,128)(2,1)S(1)} %broadcast_in_dim.28), channel_id=1, replica_groups=mesh['x'=4,'zh'=3,'zl'=4,'y'=8,'c'=2] {'x'}, dimensions={0} | all-to-all | bytes 524288 | tf_op jit(solution)/shard_map/all_to_all | solution.py:201
  65.1 2.2 %all_gather.3.gathered = bf16[512,512]{1,0:T(8,128)(2,1)S(1)} all-gather(bf16[256,512]{1,0:T(8,128)(2,1)S(1)} %bitcast.12), channel_id=1, replica_groups=mesh['x'=4,'zh'=3,'zl'=4,'y'=8,'c'=2] {'c'}, dimensions={0}, use_global_device_ids=true | all-gather | bytes 786432 | tf_op jit(solution)/shard_map/all_gather | solution.py:229
  67.3 0.7 tiles.1
  68.0 0.1 reshape.52
  68.0 14.9 %all_to_all.28 = bf16[32,4,768]{2,1,0:T(4,128)(2,1)S(1)} all-to-all(bf16[32,4,768]{2,1,0:T(4,128)(2,1)S(1)} %reshape.52), channel_id=1, replica_groups=mesh['x'=4,'zh'=3,'zl'=4,'y'=8,'c'=2] {'zl','y'}, dimensions={0} | all-to-all | bytes 393216 | tf_op jit(solution)/shard_map/all_to_all | solution.py:201
  82.9 0.1 reshape.53.parts
  82.9 0.2 sums.1
  83.2 14.7 %all_to_all.29 = bf16[12,4,512]{2,1,0:T(4,128)(2,1)S(1)} all-to-all(bf16[12,4,512]{2,1,0:T(4,128)(2,1)S(1)} %reshape.54), channel_id=1, replica_groups=mesh['x'=4,'zh'=3,'zl'=4,'y'=8,'c'=2] {'x','zh'}, dimensions={0} | all-to-all | bytes 98304 | tf_op jit(solution)/shard_map/all_to_all | solution.py:201
  97.9 0.8 results.1
  (13 shorter events, 0.2 us)
Async XLA Ops:
  0.6 1.0 %copy-start.6 = (bf16[8,6,16,32]{3,2,1,0:T(8,128)(2,1)S(1)}, bf16[8,6,16,32]{3,2,1,0:T(8,128)(2,1)}, u32[]{:S(2)}) copy-start(bf16[8,6,16,32]{3,2,1,0:T(8,128)(2,1)} %param.8) | copy-start | bytes 147460
  1.7 28.6 %copy-start.2 = (bf16[656,96]{1,0:T(8,128)(2,1)S(1)}, bf16[656,96]{1,0:T(8,128)(2,1)}, u32[]{:S(2)}) copy-start(bf16[656,96]{1,0:T(8,128)(2,1)} %constant.16.clone.unpack_rows) | copy-start | bytes 377860
  1.7 28.6 %copy-start.4 = (bf16[144,144]{1,0:T(8,128)(2,1)S(1)}, bf16[144,144]{1,0:T(8,128)(2,1)}, u32[]{:S(2)}) copy-start(bf16[144,144]{1,0:T(8,128)(2,1)} %constant.19.clone.high_z) | copy-start | bytes 124420
  1.9 28.4 %copy-start.3 = (bf16[144,144]{1,0:T(8,128)(2,1)S(1)}, bf16[144,144]{1,0:T(8,128)(2,1)}, u32[]{:S(2)}) copy-start(bf16[144,144]{1,0:T(8,128)(2,1)} %constant.20.clone.low_z) | copy-start | bytes 124420
  1.9 28.4 %copy-start = (bf16[512,512]{1,0:T(8,128)(2,1)S(1)}, bf16[512,512]{1,0:T(8,128)(2,1)}, u32[]{:S(2)}) copy-start(bf16[512,512]{1,0:T(8,128)(2,1)} %constant.18.clone.low_xy) | copy-start | bytes 1572868
  1.9 28.4 %copy-start.1 = (bf16[512,512]{1,0:T(8,128)(2,1)S(1)}, bf16[512,512]{1,0:T(8,128)(2,1)}, u32[]{:S(2)}) copy-start(bf16[512,512]{1,0:T(8,128)(2,1)} %constant.17.clone.high_xy) | copy-start | bytes 1572868
  30.3 0.7 copy-start.5

commit v8 on v7

--- a/solution.py
+++ b/solution.py
@@ -80,6 +80,10 @@
 unpack = unpacking()
 
 
+def slab_of(line):
+    return sum(jnp.where(line >= THICK * slab, 1, 0) for slab in range(1, 4))
+
+
 def product(a, b):
     return lax.dot_general(a, b, (((1,), (0,)), ((), ())), preferred_element_type=f32)
 
@@ -115,8 +119,9 @@
 
     row = lax.broadcasted_iota(jnp.int32, (48, count), 0)
     col = lax.broadcasted_iota(jnp.int32, (48, count), 1)
-    group = (row >> 1) & 7
-    z = THICK * (3 * (group >> 1) + lax.axis_index("zh")) + 3 * (group & 1) + (row >> 4)
+    line = ((row >> 1) & 7) + 8 * (row >> 4)
+    slab = slab_of(line)
+    z = THICK * (3 * slab + lax.axis_index("zh")) + line - THICK * slab
     pick = jnp.where(col == (row & 1) * NZ + z, 1.0, 0.0).astype(bf16)
     filtered_rows = product(pick, current).astype(bf16)
     applied_rows = product(pick, applied).astype(bf16)
@@ -161,13 +166,14 @@
         left, states.astype(bf16), (((1,), (1,)), ((), ())), preferred_element_type=f32
     )
     out[:, 0:512] = tiles.astype(bf16)
+    cells = jnp.zeros((1, 128), f32)
+    for p in range(3):
+        mine = slab_of(lax.axis_index("y") + 8 * p) == lax.axis_index("x")
+        cells = jnp.where(mine, density[:, p * 128 : p * 128 + 128], cells)
+    high = cells.astype(bf16).astype(f32)
     kind = row & 3
-    block = jnp.zeros((128, 128), f32)
-    for p in range(3):
-        block = jnp.where(kind == p, density[:, p * 128 : p * 128 + 128], block)
-    high = block.astype(bf16)
-    out[:, 512:640] = high
-    out[:, 640:768] = (block - high.astype(f32)).astype(bf16)
+    block = jnp.where(kind == 0, high, jnp.where(kind == 1, cells - high, 0.0))
+    out[:, 512:640] = block.astype(bf16)
 
 
 def sum_kernel(parts, rows, density):
@@ -177,12 +183,12 @@
     rows[...] = product(adder, parts[:, 0:512]).astype(bf16)
     row = lax.broadcasted_iota(jnp.int32, (8, 128), 0)
     col = lax.broadcasted_iota(jnp.int32, (8, 128), 1)
-    half = jnp.where(row >= 3, 1, 0)
     for lane_block in range(4):
-        sender = lane_block * 8 + 2 * lax.axis_index("x") + half
-        pick = jnp.where((col == sender * 4 + row - 3 * half) & (row < THICK), 1.0, 0.0).astype(bf16)
+        sender = lane_block * 8 + ((THICK * lax.axis_index("x") + row) & 7)
+        hit = ((col == sender * 4) | (col == sender * 4 + 1)) & (row < THICK)
+        pick = jnp.where(hit, 1.0, 0.0).astype(bf16)
         lanes = slice(lane_block * 128, lane_block * 128 + 128)
-        density[:, lanes] = product(pick, parts[:, 512:640]) + product(pick, parts[:, 640:768])
+        density[:, lanes] = product(pick, parts[:, 512:640])
 
 
 def final_kernel(received, cells, energy, gram, density):
@@ -230,14 +236,14 @@
 
     partial = pl.pallas_call(
         tile_kernel,
-        out_shape=jax.ShapeDtypeStruct((128, 768), bf16),
+        out_shape=jax.ShapeDtypeStruct((128, 640), bf16),
         in_specs=[vmem] * 2,
         out_specs=vmem,
         compiler_params=params,
         name="tiles",
     )(own, gathered)
 
-    parts = exchange(partial.reshape(32, 4, 768), ("zl", "y")).reshape(128, 768)
+    parts = exchange(partial.reshape(32, 4, 640), ("zl", "y")).reshape(128, 640)
     rows, cells = pl.pallas_call(
         sum_kernel,
         out_shape=[

time: 99 us -> 98.3 us (level)
  no operation moved by 1% of the time
where the time goes in v8:
time: 98.3 us; the launch traced here: 98 us
  blocking collectives  91.3 us (93%)
  Pallas kernels  3.73 us (4%)
  local copies, waits for them, and re-layouts  1.27 us (1%)
    all_to_all x5, blocking collectives, exchange(): return lax.all_to_all(array, axes, 0, 0, tiled=True)  89.1 us
    all_gather x1, blocking collectives, body(): gathered = lax.all_gather(gathered, 'c', axis=0, tiled=True)  2.17 us
    pallas_call x1, Pallas kernels, body(): pl.pallas_call(filter_kernel, out_shape=jax.ShapeDtypeStruct((64, 896), b...  2.12 us

profile of v8, /device:TPU:8, one launch (start us, length us, event | category | flops | bytes accessed | tf_op | source)
XLA Modules:
  0.0 98.0 jit_solution(3782287976706327876)
XLA Ops:
  0.6 0.0 copy-start.6
  0.6 0.9 fusion.2
  1.5 0.1 broadcast_in_dim.23
  1.7 0.0 copy-done.6
  1.7 0.0 copy-start.2
  1.7 0.0 copy-start.4
  1.7 0.2 reshape.46
  1.9 0.0 copy-start.3
  1.9 0.0 copy-start
  1.9 0.0 copy-start.1
  2.0 28.3 %all_to_all.25 = bf16[12,8,1152]{2,1,0:T(8,128)(2,1)S(1)} all-to-all(bf16[12,8,1152]{2,1,0:T(8,128)(2,1)S(1)} %bitcast.13), channel_id=1, replica_groups=mesh['x'=4,'zh'=3,'zl'=4,'y'=8,'c'=2] {'x','zh'}, dimensions={0} | all-to-all | bytes 442368 | tf_op jit(solution)/shard_map/all_to_all | solution.py:207
  30.3 0.0 copy-start.5
  30.3 0.0 copy-done.2
  30.3 0.0 copy-done.4
  30.3 0.0 copy-done.3
  30.3 0.0 copy-done
  30.3 0.0 copy-done.1
  30.3 0.6 copy-done.5
  30.9 2.1 %chebyshev.1 = bf16[64,896]{1,0:T(8,128)(2,1)S(1)} custom-call(f32[1,8]{1,0:T(1,128)S(1)} %bitcast.11, bf16[96,1152]{1,0:T(8,128)(2,1)S(1)} %bitcast.10, bf16[656,96]{1,0:T(8,128)(2,1)S(1)} %copy-done.2, bf16[512,512]{1,0:T(8,128)(2,1)S(1)} %copy-done.1, bf16[512,512]{1,0:T(8,128)(2,1)S(1)} %copy-done, bf16[144,144]{1,0:T(8,128)(2,1)S(1)} %copy-done.4, ...), custom_call_target="tpu_custom_call" | custom-call | tf_op jit(solution)/shard_map/chebyshev/pallas_call | solution.py:223
  33.1 0.1 reshape.49
  33.1 22.8 %all_to_all.26 = bf16[32,2,896]{2,1,0:T(2,128)(2,1)S(1)} all-to-all(bf16[32,2,896]{2,1,0:T(2,128)(2,1)S(1)} %reshape.49), channel_id=1, replica_groups=mesh['x'=4,'zh'=3,'zl'=4,'y'=8,'c'=2] {'zl','y'}, dimensions={0} | all-to-all | bytes 229376 | tf_op jit(solution)/shard_map/all_to_all | solution.py:207
  56.0 9.1 %all_to_all.27 = bf16[4,64,512]{2,1,0:T(8,128)(2,1)S(1)} all-to-all(bf16[4,64,512]{2,1,0:T(8,128)(2,1)S(1)} %broadcast_in_dim.28), channel_id=1, replica_groups=mesh['x'=4,'zh'=3,'zl'=4,'y'=8,'c'=2] {'x'}, dimensions={0} | all-to-all | bytes 524288 | tf_op jit(solution)/shard_map/all_to_all | solution.py:207
  65.1 2.2 %all_gather.3.gathered = bf16[512,512]{1,0:T(8,128)(2,1)S(1)} all-gather(bf16[256,512]{1,0:T(8,128)(2,1)S(1)} %bitcast.12), channel_id=1, replica_groups=mesh['x'=4,'zh'=3,'zl'=4,'y'=8,'c'=2] {'c'}, dimensions={0}, use_global_device_ids=true | all-gather | bytes 786432 | tf_op jit(solution)/shard_map/all_gather | solution.py:235
  67.3 0.7 tiles.1
  68.0 14.2 %all_to_all.28 = bf16[32,4,640]{2,1,0:T(4,128)(2,1)S(1)} all-to-all(bf16[32,4,640]{2,1,0:T(4,128)(2,1)S(1)} %reshape.52), channel_id=1, replica_groups=mesh['x'=4,'zh'=3,'zl'=4,'y'=8,'c'=2] {'zl','y'}, dimensions={0} | all-to-all | bytes 327680 | tf_op jit(solution)/shard_map/all_to_all | solution.py:207
  82.3 0.2 sums.1
  82.5 14.7 %all_to_all.29 = bf16[12,4,512]{2,1,0:T(4,128)(2,1)S(1)} all-to-all(bf16[12,4,512]{2,1,0:T(4,128)(2,1)S(1)} %reshape.54), channel_id=1, replica_groups=mesh['x'=4,'zh'=3,'zl'=4,'y'=8,'c'=2] {'x','zh'}, dimensions={0} | all-to-all | bytes 98304 | tf_op jit(solution)/shard_map/all_to_all | solution.py:207
  97.2 0.8 results.1
  (15 shorter events, 0.3 us)
Async XLA Ops:
  0.6 1.0 %copy-start.6 = (bf16[8,6,16,32]{3,2,1,0:T(8,128)(2,1)S(1)}, bf16[8,6,16,32]{3,2,1,0:T(8,128)(2,1)}, u32[]{:S(2)}) copy-start(bf16[8,6,16,32]{3,2,1,0:T(8,128)(2,1)} %param.8) | copy-start | bytes 147460
  1.7 28.6 %copy-start.2 = (bf16[656,96]{1,0:T(8,128)(2,1)S(1)}, bf16[656,96]{1,0:T(8,128)(2,1)}, u32[]{:S(2)}) copy-start(bf16[656,96]{1,0:T(8,128)(2,1)} %constant.16.clone.unpack_rows) | copy-start | bytes 377860
  1.7 28.6 %copy-start.4 = (bf16[144,144]{1,0:T(8,128)(2,1)S(1)}, bf16[144,144]{1,0:T(8,128)(2,1)}, u32[]{:S(2)}) copy-start(bf16[144,144]{1,0:T(8,128)(2,1)} %constant.19.clone.high_z) | copy-start | bytes 124420
  1.9 28.4 %copy-start.3 = (bf16[144,144]{1,0:T(8,128)(2,1)S(1)}, bf16[144,144]{1,0:T(8,128)(2,1)}, u32[]{:S(2)}) copy-start(bf16[144,144]{1,0:T(8,128)(2,1)} %constant.20.clone.low_z) | copy-start | bytes 124420
  1.9 28.4 %copy-start = (bf16[512,512]{1,0:T(8,128)(2,1)S(1)}, bf16[512,512]{1,0:T(8,128)(2,1)}, u32[]{:S(2)}) copy-start(bf16[512,512]{1,0:T(8,128)(2,1)} %constant.18.clone.low_xy) | copy-start | bytes 1572868
  1.9 28.4 %copy-start.1 = (bf16[512,512]{1,0:T(8,128)(2,1)S(1)}, bf16[512,512]{1,0:T(8,128)(2,1)}, u32[]{:S(2)}) copy-start(bf16[512,512]{1,0:T(8,128)(2,1)} %constant.17.clone.high_xy) | copy-start | bytes 1572868
  30.3 0.7 copy-start.5

commit v9 on v8

--- a/solution.py
+++ b/solution.py
@@ -132,28 +132,34 @@
             target = slice(lane_block * 16, lane_block * 16 + 16)
             out[target, p * 128 : p * 128 + 128] = filtered_rows[rows, lanes]
             out[target, 512 + p * 128 : 640 + p * 128] = applied_rows[rows, lanes]
-    state = lax.broadcasted_iota(jnp.int32, (64, 128), 0) & 1
-    lane = lax.broadcasted_iota(jnp.int32, (64, 128), 1)
-    held = lax.broadcasted_iota(jnp.int32, (1, 8), 1)
-    mine = 2 * lax.axis_index("x")
-    block = jnp.zeros((64, 128), f32)
-    for k in range(2):
-        value = jnp.sum(jnp.where(held == mine + k, occupation[...], 0.0), axis=1, keepdims=True)
-        for piece in range(3):
-            part = value.astype(bf16).astype(f32)
-            value = value - part
-            block = jnp.where((lane == piece) & (state == k), part, block)
-    out[:, 384:512] = block.astype(bf16)
+    lane = lax.broadcasted_iota(jnp.int32, (8, 128), 1)
+    held = lax.broadcasted_iota(jnp.int32, (8, 128), 0)
+    value = jnp.sum(
+        jnp.where(held[:, 0:8] == lane[:, 0:8], occupation[...], 0.0), axis=1, keepdims=True
+    )
+    block = jnp.zeros((8, 128), f32)
+    for piece in range(3):
+        part = value.astype(bf16).astype(f32)
+        value = value - part
+        block = jnp.where(lane == 8 * piece + held, part, block)
+    block = jnp.sum(block, axis=0, keepdims=True)
+    out[:, 384:512] = jnp.broadcast_to(block, (64, 128)).astype(bf16)
 
 
 def tile_kernel(own, gathered, out):
     row = lax.broadcasted_iota(jnp.int32, (NS, NS), 0)
     col = lax.broadcasted_iota(jnp.int32, (NS, NS), 1)
-    source = ((((row >> 3) & 1) * 4 + ((row >> 1) & 3)) * 32 + (row >> 4)) * 2 + (row & 1)
+    source = ((row >> 3) & 1) * 256 + ((row >> 1) & 3) * 64 + (row >> 4) * 2 + (row & 1)
     order = jnp.where(col == source, 1.0, 0.0).astype(bf16)
-    ordered = product(order, gathered[...])
-    states = ordered[:, :384]
-    occupied = ordered[:, 384:385] + ordered[:, 385:386] + ordered[:, 386:387]
+    states = product(order, jnp.concatenate([gathered[0:256], gathered[320:576]], axis=0))
+    held = lax.broadcasted_iota(jnp.int32, (NS, 128), 0)
+    lane = lax.broadcasted_iota(jnp.int32, (NS, 128), 1)
+    owner = jnp.where(lane == ((held >> 3) & 1) * 64 + (held >> 4) * 2, 1.0, 0.0).astype(bf16)
+    pieces = product(
+        owner, jnp.concatenate([gathered[256:320, 0:128], gathered[576:640, 0:128]], axis=0)
+    )
+    wanted = ((lane & 7) == (held & 7)) & (lane < 24)
+    occupied = jnp.sum(jnp.where(wanted, pieces, 0.0), axis=1, keepdims=True)
     density = jnp.sum(occupied * (states * states), axis=0, keepdims=True) * (1.0 / NS)
 
     row = lax.broadcasted_iota(jnp.int32, (128, 128), 0)
@@ -230,8 +236,11 @@
     )(occupation.reshape(1, 8), slabs, unpack, plane_high, plane_low, depth_high, depth_low)
 
     own = exchange(send.reshape(32, 2, 896), ("zl", "y")).reshape(64, 896)
-    shared = jnp.broadcast_to(own[None, :, :512], (4, 64, 512))
-    gathered = exchange(shared, "x").reshape(256, 512)
+    shared = jnp.broadcast_to(own[None, :, :384], (4, 64, 384))
+    gathered = exchange(shared, "x").reshape(256, 384)
+    gathered, late = lax.optimization_barrier((gathered, own))
+    occupied = jnp.pad(late[:, 384:512], ((0, 0), (0, 256)))
+    gathered = jnp.concatenate([gathered, occupied], axis=0)
     gathered = lax.all_gather(gathered, "c", axis=0, tiled=True)
 
     partial = pl.pallas_call(

time: 98.3 us -> 97.9 us (level)
  no operation moved by 1% of the time
where the time goes in v9:
time: 97.9 us; the launch traced here: 97.6 us
  blocking collectives  90.9 us (93%)
  Pallas kernels  3.71 us (4%)
  local copies, waits for them, and re-layouts  1.27 us (1%)
    all_to_all x5, blocking collectives, exchange(): return lax.all_to_all(array, axes, 0, 0, tiled=True)  88.7 us
    all_gather x1, blocking collectives, body(): gathered = lax.all_gather(gathered, 'c', axis=0, tiled=True)  2.16 us
    pallas_call x1, Pallas kernels, body(): pl.pallas_call(filter_kernel, out_shape=jax.ShapeDtypeStruct((64, 896), b...  2.12 us

profile of v9, /device:TPU:8, one launch (start us, length us, event | category | flops | bytes accessed | tf_op | source)
XLA Modules:
  0.0 97.6 jit_solution(14567445236956817301)
XLA Ops:
  0.6 0.0 copy-start.6
  0.6 0.9 fusion.4
  1.5 0.1 broadcast_in_dim.23
  1.7 0.0 copy-done.6
  1.7 0.0 copy-start.2
  1.7 0.0 copy-start.4
  1.7 0.2 reshape.46
  1.9 0.0 copy-start.3
  1.9 0.0 copy-start
  1.9 0.0 copy-start.1
  2.0 28.3 %all_to_all.25 = bf16[12,8,1152]{2,1,0:T(8,128)(2,1)S(1)} all-to-all(bf16[12,8,1152]{2,1,0:T(8,128)(2,1)S(1)} %bitcast.12), channel_id=1, replica_groups=mesh['x'=4,'zh'=3,'zl'=4,'y'=8,'c'=2] {'x','zh'}, dimensions={0} | all-to-all | bytes 442368 | tf_op jit(solution)/shard_map/all_to_all | solution.py:213
  30.3 0.0 copy-start.5
  30.3 0.0 copy-done.2
  30.3 0.0 copy-done.4
  30.3 0.0 copy-done.3
  30.3 0.0 copy-done
  30.3 0.0 copy-done.1
  30.3 0.6 copy-done.5
  30.9 2.1 %chebyshev.1 = bf16[64,896]{1,0:T(8,128)(2,1)S(1)} custom-call(f32[1,8]{1,0:T(1,128)S(1)} %bitcast.11, bf16[96,1152]{1,0:T(8,128)(2,1)S(1)} %bitcast.10, bf16[656,96]{1,0:T(8,128)(2,1)S(1)} %copy-done.2, bf16[512,512]{1,0:T(8,128)(2,1)S(1)} %copy-done.1, bf16[512,512]{1,0:T(8,128)(2,1)S(1)} %copy-done, bf16[144,144]{1,0:T(8,128)(2,1)S(1)} %copy-done.4, ...), custom_call_target="tpu_custom_call" | custom-call | tf_op jit(solution)/shard_map/chebyshev/pallas_call | solution.py:229
  33.1 0.1 reshape.49
  33.1 22.8 %all_to_all.26 = bf16[32,2,896]{2,1,0:T(2,128)(2,1)S(1)} all-to-all(bf16[32,2,896]{2,1,0:T(2,128)(2,1)S(1)} %reshape.49), channel_id=1, replica_groups=mesh['x'=4,'zh'=3,'zl'=4,'y'=8,'c'=2] {'zl','y'}, dimensions={0} | all-to-all | bytes 229376 | tf_op jit(solution)/shard_map/all_to_all | solution.py:213
  56.0 8.7 %all_to_all.27 = bf16[4,64,384]{2,1,0:T(8,128)(2,1)S(1)} all-to-all(bf16[4,64,384]{2,1,0:T(8,128)(2,1)S(1)} %broadcast_in_dim.28), channel_id=1, replica_groups=mesh['x'=4,'zh'=3,'zl'=4,'y'=8,'c'=2] {'x'}, dimensions={0} | all-to-all | bytes 393216 | tf_op jit(solution)/shard_map/all_to_all | solution.py:213
  64.8 2.2 %all_gather.3.gathered = bf16[640,384]{1,0:T(8,128)(2,1)S(1)} all-gather(bf16[320,384]{1,0:T(8,128)(2,1)S(1)} %fusion.1), channel_id=1, replica_groups=mesh['x'=4,'zh'=3,'zl'=4,'y'=8,'c'=2] {'c'}, dimensions={0}, use_global_device_ids=true | all-gather | bytes 737280 | tf_op jit(solution)/shard_map/all_gather | solution.py:244
  66.9 0.7 tiles.1
  67.6 14.2 %all_to_all.28 = bf16[32,4,640]{2,1,0:T(4,128)(2,1)S(1)} all-to-all(bf16[32,4,640]{2,1,0:T(4,128)(2,1)S(1)} %reshape.52), channel_id=1, replica_groups=mesh['x'=4,'zh'=3,'zl'=4,'y'=8,'c'=2] {'zl','y'}, dimensions={0} | all-to-all | bytes 327680 | tf_op jit(solution)/shard_map/all_to_all | solution.py:213
  81.9 0.2 sums.1
  82.1 14.7 %all_to_all.29 = bf16[12,4,512]{2,1,0:T(4,128)(2,1)S(1)} all-to-all(bf16[12,4,512]{2,1,0:T(4,128)(2,1)S(1)} %reshape.54), channel_id=1, replica_groups=mesh['x'=4,'zh'=3,'zl'=4,'y'=8,'c'=2] {'x','zh'}, dimensions={0} | all-to-all | bytes 98304 | tf_op jit(solution)/shard_map/all_to_all | solution.py:213
  96.8 0.8 results.1
  (17 shorter events, 0.3 us)
Async XLA Ops:
  0.6 1.0 %copy-start.6 = (bf16[8,6,16,32]{3,2,1,0:T(8,128)(2,1)S(1)}, bf16[8,6,16,32]{3,2,1,0:T(8,128)(2,1)}, u32[]{:S(2)}) copy-start(bf16[8,6,16,32]{3,2,1,0:T(8,128)(2,1)} %param.8) | copy-start | bytes 147460
  1.7 28.6 %copy-start.2 = (bf16[656,96]{1,0:T(8,128)(2,1)S(1)}, bf16[656,96]{1,0:T(8,128)(2,1)}, u32[]{:S(2)}) copy-start(bf16[656,96]{1,0:T(8,128)(2,1)} %constant.19.clone.unpack_rows) | copy-start | bytes 377860
  1.7 28.6 %copy-start.4 = (bf16[144,144]{1,0:T(8,128)(2,1)S(1)}, bf16[144,144]{1,0:T(8,128)(2,1)}, u32[]{:S(2)}) copy-start(bf16[144,144]{1,0:T(8,128)(2,1)} %constant.22.clone.high_z) | copy-start | bytes 124420
  1.9 28.4 %copy-start.3 = (bf16[144,144]{1,0:T(8,128)(2,1)S(1)}, bf16[144,144]{1,0:T(8,128)(2,1)}, u32[]{:S(2)}) copy-start(bf16[144,144]{1,0:T(8,128)(2,1)} %constant.23.clone.low_z) | copy-start | bytes 124420
  1.9 28.4 %copy-start = (bf16[512,512]{1,0:T(8,128)(2,1)S(1)}, bf16[512,512]{1,0:T(8,128)(2,1)}, u32[]{:S(2)}) copy-start(bf16[512,512]{1,0:T(8,128)(2,1)} %constant.21.clone.low_xy) | copy-start | bytes 1572868
  1.9 28.4 %copy-start.1 = (bf16[512,512]{1,0:T(8,128)(2,1)S(1)}, bf16[512,512]{1,0:T(8,128)(2,1)}, u32[]{:S(2)}) copy-start(bf16[512,512]{1,0:T(8,128)(2,1)} %constant.20.clone.high_xy) | copy-start | bytes 1572868
  30.3 0.7 copy-start.5

commit v10 on v9

--- a/solution.py
+++ b/solution.py
@@ -160,7 +160,11 @@
     )
     wanted = ((lane & 7) == (held & 7)) & (lane < 24)
     occupied = jnp.sum(jnp.where(wanted, pieces, 0.0), axis=1, keepdims=True)
-    density = jnp.sum(occupied * (states * states), axis=0, keepdims=True) * (1.0 / NS)
+    cells = jnp.zeros((NS, 128), f32)
+    for p in range(3):
+        mine = slab_of(lax.axis_index("y") + 8 * p) == lax.axis_index("x")
+        cells = jnp.where(mine, states[:, p * 128 : p * 128 + 128], cells)
+    density = jnp.sum(occupied * (cells * cells), axis=0, keepdims=True) * (1.0 / NS)
 
     row = lax.broadcasted_iota(jnp.int32, (128, 128), 0)
     col = lax.broadcasted_iota(jnp.int32, (128, 128), 1)
@@ -172,13 +176,9 @@
         left, states.astype(bf16), (((1,), (1,)), ((), ())), preferred_element_type=f32
     )
     out[:, 0:512] = tiles.astype(bf16)
-    cells = jnp.zeros((1, 128), f32)
-    for p in range(3):
-        mine = slab_of(lax.axis_index("y") + 8 * p) == lax.axis_index("x")
-        cells = jnp.where(mine, density[:, p * 128 : p * 128 + 128], cells)
-    high = cells.astype(bf16).astype(f32)
+    high = density.astype(bf16).astype(f32)
     kind = row & 3
-    block = jnp.where(kind == 0, high, jnp.where(kind == 1, cells - high, 0.0))
+    block = jnp.where(kind == 0, high, jnp.where(kind == 1, density - high, 0.0))
     out[:, 512:640] = block.astype(bf16)
 
 

time: 97.9 us -> 97.9 us (level)
  no operation moved by 1% of the time
where the time goes in v10:
time: 97.9 us; the launch traced here: 97.6 us
  blocking collectives  90.9 us (93%)
  Pallas kernels  3.71 us (4%)
  local copies, waits for them, and re-layouts  1.27 us (1%)
    all_to_all x5, blocking collectives, exchange(): return lax.all_to_all(array, axes, 0, 0, tiled=True)  88.7 us
    all_gather x1, blocking collectives, body(): gathered = lax.all_gather(gathered, 'c', axis=0, tiled=True)  2.16 us
    pallas_call x1, Pallas kernels, body(): pl.pallas_call(filter_kernel, out_shape=jax.ShapeDtypeStruct((64, 896), b...  2.12 us

profile of v10, /device:TPU:8, one launch (start us, length us, event | category | flops | bytes accessed | tf_op | source)
XLA Modules:
  0.0 97.6 jit_solution(2397312980274948283)
XLA Ops:
  0.6 0.0 copy-start.6
  0.6 0.9 fusion.4
  1.5 0.1 broadcast_in_dim.23
  1.7 0.0 copy-done.6
  1.7 0.0 copy-start.2
  1.7 0.0 copy-start.4
  1.7 0.2 reshape.46
  1.9 0.0 copy-start.3
  1.9 0.0 copy-start
  1.9 0.0 copy-start.1
  2.0 28.3 %all_to_all.25 = bf16[12,8,1152]{2,1,0:T(8,128)(2,1)S(1)} all-to-all(bf16[12,8,1152]{2,1,0:T(8,128)(2,1)S(1)} %bitcast.12), channel_id=1, replica_groups=mesh['x'=4,'zh'=3,'zl'=4,'y'=8,'c'=2] {'x','zh'}, dimensions={0} | all-to-all | bytes 442368 | tf_op jit(solution)/shard_map/all_to_all | solution.py:213
  30.3 0.0 copy-start.5
  30.3 0.0 copy-done.2
  30.3 0.0 copy-done.4
  30.3 0.0 copy-done.3
  30.3 0.0 copy-done
  30.3 0.0 copy-done.1
  30.3 0.6 copy-done.5
  30.9 2.1 %chebyshev.1 = bf16[64,896]{1,0:T(8,128)(2,1)S(1)} custom-call(f32[1,8]{1,0:T(1,128)S(1)} %bitcast.11, bf16[96,1152]{1,0:T(8,128)(2,1)S(1)} %bitcast.10, bf16[656,96]{1,0:T(8,128)(2,1)S(1)} %copy-done.2, bf16[512,512]{1,0:T(8,128)(2,1)S(1)} %copy-done.1, bf16[512,512]{1,0:T(8,128)(2,1)S(1)} %copy-done, bf16[144,144]{1,0:T(8,128)(2,1)S(1)} %copy-done.4, ...), custom_call_target="tpu_custom_call" | custom-call | tf_op jit(solution)/shard_map/chebyshev/pallas_call | solution.py:229
  33.1 0.1 reshape.49
  33.1 22.8 %all_to_all.26 = bf16[32,2,896]{2,1,0:T(2,128)(2,1)S(1)} all-to-all(bf16[32,2,896]{2,1,0:T(2,128)(2,1)S(1)} %reshape.49), channel_id=1, replica_groups=mesh['x'=4,'zh'=3,'zl'=4,'y'=8,'c'=2] {'zl','y'}, dimensions={0} | all-to-all | bytes 229376 | tf_op jit(solution)/shard_map/all_to_all | solution.py:213
  56.0 8.7 %all_to_all.27 = bf16[4,64,384]{2,1,0:T(8,128)(2,1)S(1)} all-to-all(bf16[4,64,384]{2,1,0:T(8,128)(2,1)S(1)} %broadcast_in_dim.28), channel_id=1, replica_groups=mesh['x'=4,'zh'=3,'zl'=4,'y'=8,'c'=2] {'x'}, dimensions={0} | all-to-all | bytes 393216 | tf_op jit(solution)/shard_map/all_to_all | solution.py:213
  64.8 2.2 %all_gather.3.gathered = bf16[640,384]{1,0:T(8,128)(2,1)S(1)} all-gather(bf16[320,384]{1,0:T(8,128)(2,1)S(1)} %fusion.1), channel_id=1, replica_groups=mesh['x'=4,'zh'=3,'zl'=4,'y'=8,'c'=2] {'c'}, dimensions={0}, use_global_device_ids=true | all-gather | bytes 737280 | tf_op jit(solution)/shard_map/all_gather | solution.py:244
  66.9 0.7 tiles.1
  67.6 14.2 %all_to_all.28 = bf16[32,4,640]{2,1,0:T(4,128)(2,1)S(1)} all-to-all(bf16[32,4,640]{2,1,0:T(4,128)(2,1)S(1)} %reshape.52), channel_id=1, replica_groups=mesh['x'=4,'zh'=3,'zl'=4,'y'=8,'c'=2] {'zl','y'}, dimensions={0} | all-to-all | bytes 327680 | tf_op jit(solution)/shard_map/all_to_all | solution.py:213
  81.9 0.2 sums.1
  82.1 14.7 %all_to_all.29 = bf16[12,4,512]{2,1,0:T(4,128)(2,1)S(1)} all-to-all(bf16[12,4,512]{2,1,0:T(4,128)(2,1)S(1)} %reshape.54), channel_id=1, replica_groups=mesh['x'=4,'zh'=3,'zl'=4,'y'=8,'c'=2] {'x','zh'}, dimensions={0} | all-to-all | bytes 98304 | tf_op jit(solution)/shard_map/all_to_all | solution.py:213
  96.8 0.8 results.1
  (17 shorter events, 0.3 us)
Async XLA Ops:
  0.6 1.0 %copy-start.6 = (bf16[8,6,16,32]{3,2,1,0:T(8,128)(2,1)S(1)}, bf16[8,6,16,32]{3,2,1,0:T(8,128)(2,1)}, u32[]{:S(2)}) copy-start(bf16[8,6,16,32]{3,2,1,0:T(8,128)(2,1)} %param.8) | copy-start | bytes 147460
  1.7 28.6 %copy-start.2 = (bf16[656,96]{1,0:T(8,128)(2,1)S(1)}, bf16[656,96]{1,0:T(8,128)(2,1)}, u32[]{:S(2)}) copy-start(bf16[656,96]{1,0:T(8,128)(2,1)} %constant.19.clone.unpack_rows) | copy-start | bytes 377860
  1.7 28.6 %copy-start.4 = (bf16[144,144]{1,0:T(8,128)(2,1)S(1)}, bf16[144,144]{1,0:T(8,128)(2,1)}, u32[]{:S(2)}) copy-start(bf16[144,144]{1,0:T(8,128)(2,1)} %constant.22.clone.high_z) | copy-start | bytes 124420
  1.9 28.4 %copy-start.3 = (bf16[144,144]{1,0:T(8,128)(2,1)S(1)}, bf16[144,144]{1,0:T(8,128)(2,1)}, u32[]{:S(2)}) copy-start(bf16[144,144]{1,0:T(8,128)(2,1)} %constant.23.clone.low_z) | copy-start | bytes 124420
  1.9 28.4 %copy-start = (bf16[512,512]{1,0:T(8,128)(2,1)S(1)}, bf16[512,512]{1,0:T(8,128)(2,1)}, u32[]{:S(2)}) copy-start(bf16[512,512]{1,0:T(8,128)(2,1)} %constant.21.clone.low_xy) | copy-start | bytes 1572868
  1.9 28.4 %copy-start.1 = (bf16[512,512]{1,0:T(8,128)(2,1)S(1)}, bf16[512,512]{1,0:T(8,128)(2,1)}, u32[]{:S(2)}) copy-start(bf16[512,512]{1,0:T(8,128)(2,1)} %constant.20.clone.high_xy) | copy-start | bytes 1572868
  30.3 0.7 copy-start.5

commit v11 on v10

--- a/solution.py
+++ b/solution.py
@@ -43,8 +43,8 @@
     line = np.zeros((count, count))
     rows = np.arange(count)
     for reach in range(1, RADIUS + 1):
-        line[rows, (rows + reach) % count] += -0.5 * stencil_weights[reach]
-        line[rows, (rows - reach) % count] += -0.5 * stencil_weights[reach]
+        line[rows, (rows + reach) % count] += -stencil_weights[reach] / spread
+        line[rows, (rows - reach) % count] += -stencil_weights[reach] / spread
     return line
 
 
@@ -98,7 +98,7 @@
     )
     levels = jnp.log(code) * (1.0 / (CODE * math.log(2.0))) - OFFSET - 1.5 * stencil_weights[0]
     diagonal = jnp.concatenate([levels, levels], axis=0)
-    shifted = diagonal - centre
+    shifted = (diagonal - centre) * (2.0 / spread)
 
     def hop(v):
         return (
@@ -109,13 +109,13 @@
         )
 
     previous = first
-    current = ((hop(first.astype(bf16)) + shifted * first) * (1.0 / spread)).astype(bf16)
+    current = ((hop(first.astype(bf16)) + shifted * first) * 0.5).astype(bf16)
     for _ in range(1, DEGREE):
         wide = current.astype(f32)
-        following = (hop(current) + shifted * wide) * (2.0 / spread) - previous
+        following = hop(current) + shifted * wide - previous
         previous = wide
         current = following.astype(bf16)
-    applied = (hop(current) + diagonal * current.astype(f32)).astype(bf16)
+    applied = (hop(current) * (0.5 * spread) + diagonal * current.astype(f32)).astype(bf16)
 
     row = lax.broadcasted_iota(jnp.int32, (48, count), 0)
     col = lax.broadcasted_iota(jnp.int32, (48, count), 1)

time: 97.9 us -> 97.9 us (level)
  no operation moved by 1% of the time
where the time goes in v11:
time: 97.9 us; the launch traced here: 97.5 us
  blocking collectives  90.9 us (93%)
  Pallas kernels  3.68 us (4%)
  local copies, waits for them, and re-layouts  1.27 us (1%)
    all_to_all x5, blocking collectives, exchange(): return lax.all_to_all(array, axes, 0, 0, tiled=True)  88.7 us
    all_gather x1, blocking collectives, body(): gathered = lax.all_gather(gathered, 'c', axis=0, tiled=True)  2.16 us
    pallas_call x1, Pallas kernels, body(): pl.pallas_call(filter_kernel, out_shape=jax.ShapeDtypeStruct((64, 896), b...  2.08 us

profile of v11, /device:TPU:8, one launch (start us, length us, event | category | flops | bytes accessed | tf_op | source)
XLA Modules:
  0.0 97.5 jit_solution(12465818367510596399)
XLA Ops:
  0.6 0.0 copy-start.6
  0.6 0.9 fusion.4
  1.5 0.1 broadcast_in_dim.23
  1.7 0.0 copy-done.6
  1.7 0.0 copy-start.2
  1.7 0.0 copy-start.4
  1.7 0.2 reshape.46
  1.9 0.0 copy-start.3
  1.9 0.0 copy-start
  1.9 0.0 copy-start.1
  2.0 28.3 %all_to_all.25 = bf16[12,8,1152]{2,1,0:T(8,128)(2,1)S(1)} all-to-all(bf16[12,8,1152]{2,1,0:T(8,128)(2,1)S(1)} %bitcast.12), channel_id=1, replica_groups=mesh['x'=4,'zh'=3,'zl'=4,'y'=8,'c'=2] {'x','zh'}, dimensions={0} | all-to-all | bytes 442368 | tf_op jit(solution)/shard_map/all_to_all | solution.py:213
  30.3 0.0 copy-start.5
  30.3 0.0 copy-done.2
  30.3 0.0 copy-done.4
  30.3 0.0 copy-done.3
  30.3 0.0 copy-done
  30.3 0.0 copy-done.1
  30.3 0.6 copy-done.5
  30.9 2.1 %chebyshev.1 = bf16[64,896]{1,0:T(8,128)(2,1)S(1)} custom-call(f32[1,8]{1,0:T(1,128)S(1)} %bitcast.11, bf16[96,1152]{1,0:T(8,128)(2,1)S(1)} %bitcast.10, bf16[656,96]{1,0:T(8,128)(2,1)S(1)} %copy-done.2, bf16[512,512]{1,0:T(8,128)(2,1)S(1)} %copy-done.1, bf16[512,512]{1,0:T(8,128)(2,1)S(1)} %copy-done, bf16[144,144]{1,0:T(8,128)(2,1)S(1)} %copy-done.4, ...), custom_call_target="tpu_custom_call" | custom-call | tf_op jit(solution)/shard_map/chebyshev/pallas_call | solution.py:229
  33.0 0.1 reshape.49
  33.1 22.8 %all_to_all.26 = bf16[32,2,896]{2,1,0:T(2,128)(2,1)S(1)} all-to-all(bf16[32,2,896]{2,1,0:T(2,128)(2,1)S(1)} %reshape.49), channel_id=1, replica_groups=mesh['x'=4,'zh'=3,'zl'=4,'y'=8,'c'=2] {'zl','y'}, dimensions={0} | all-to-all | bytes 229376 | tf_op jit(solution)/shard_map/all_to_all | solution.py:213
  56.0 8.7 %all_to_all.27 = bf16[4,64,384]{2,1,0:T(8,128)(2,1)S(1)} all-to-all(bf16[4,64,384]{2,1,0:T(8,128)(2,1)S(1)} %broadcast_in_dim.28), channel_id=1, replica_groups=mesh['x'=4,'zh'=3,'zl'=4,'y'=8,'c'=2] {'x'}, dimensions={0} | all-to-all | bytes 393216 | tf_op jit(solution)/shard_map/all_to_all | solution.py:213
  64.7 2.2 %all_gather.3.gathered = bf16[640,384]{1,0:T(8,128)(2,1)S(1)} all-gather(bf16[320,384]{1,0:T(8,128)(2,1)S(1)} %fusion.1), channel_id=1, replica_groups=mesh['x'=4,'zh'=3,'zl'=4,'y'=8,'c'=2] {'c'}, dimensions={0}, use_global_device_ids=true | all-gather | bytes 737280 | tf_op jit(solution)/shard_map/all_gather | solution.py:244
  66.9 0.7 tiles.1
  67.6 14.2 %all_to_all.28 = bf16[32,4,640]{2,1,0:T(4,128)(2,1)S(1)} all-to-all(bf16[32,4,640]{2,1,0:T(4,128)(2,1)S(1)} %reshape.52), channel_id=1, replica_groups=mesh['x'=4,'zh'=3,'zl'=4,'y'=8,'c'=2] {'zl','y'}, dimensions={0} | all-to-all | bytes 327680 | tf_op jit(solution)/shard_map/all_to_all | solution.py:213
  81.9 0.2 sums.1
  82.1 14.7 %all_to_all.29 = bf16[12,4,512]{2,1,0:T(4,128)(2,1)S(1)} all-to-all(bf16[12,4,512]{2,1,0:T(4,128)(2,1)S(1)} %reshape.54), channel_id=1, replica_groups=mesh['x'=4,'zh'=3,'zl'=4,'y'=8,'c'=2] {'x','zh'}, dimensions={0} | all-to-all | bytes 98304 | tf_op jit(solution)/shard_map/all_to_all | solution.py:213
  96.8 0.8 results.1
  (17 shorter events, 0.3 us)
Async XLA Ops:
  0.6 1.0 %copy-start.6 = (bf16[8,6,16,32]{3,2,1,0:T(8,128)(2,1)S(1)}, bf16[8,6,16,32]{3,2,1,0:T(8,128)(2,1)}, u32[]{:S(2)}) copy-start(bf16[8,6,16,32]{3,2,1,0:T(8,128)(2,1)} %param.8) | copy-start | bytes 147460
  1.7 28.6 %copy-start.2 = (bf16[656,96]{1,0:T(8,128)(2,1)S(1)}, bf16[656,96]{1,0:T(8,128)(2,1)}, u32[]{:S(2)}) copy-start(bf16[656,96]{1,0:T(8,128)(2,1)} %constant.19.clone.unpack_rows) | copy-start | bytes 377860
  1.7 28.6 %copy-start.4 = (bf16[144,144]{1,0:T(8,128)(2,1)S(1)}, bf16[144,144]{1,0:T(8,128)(2,1)}, u32[]{:S(2)}) copy-start(bf16[144,144]{1,0:T(8,128)(2,1)} %constant.22.clone.high_z) | copy-start | bytes 124420
  1.9 28.4 %copy-start.3 = (bf16[144,144]{1,0:T(8,128)(2,1)S(1)}, bf16[144,144]{1,0:T(8,128)(2,1)}, u32[]{:S(2)}) copy-start(bf16[144,144]{1,0:T(8,128)(2,1)} %constant.23.clone.low_z) | copy-start | bytes 124420
  1.9 28.4 %copy-start = (bf16[512,512]{1,0:T(8,128)(2,1)S(1)}, bf16[512,512]{1,0:T(8,128)(2,1)}, u32[]{:S(2)}) copy-start(bf16[512,512]{1,0:T(8,128)(2,1)} %constant.21.clone.low_xy) | copy-start | bytes 1572868
  1.9 28.4 %copy-start.1 = (bf16[512,512]{1,0:T(8,128)(2,1)S(1)}, bf16[512,512]{1,0:T(8,128)(2,1)}, u32[]{:S(2)}) copy-start(bf16[512,512]{1,0:T(8,128)(2,1)} %constant.20.clone.high_xy) | copy-start | bytes 1572868
  30.3 0.7 copy-start.5
